TPU v7x, 512 devices: a whole 4x8x8 slice. The times are simulated.
512 devices in a mesh: region: 16 (over y, core), sub: 32 (over x, z).
Axes of the slice: x: 4, y: 8, z: 8, core: 2. Of those that a mesh axis runs over, the one named last changes fastest.
Arguments:
- feat: bfloat16 [65536, 1024], P(('region', 'sub')), may hold values from -6 to 6
- cotangent: bfloat16 [65536, 1024], P(('region', 'sub')), may hold values from -6 to 6
- weight: bfloat16 [1024, 1024], P('sub'), may hold values from -0.1875 to 0.1875
- nbr_index: int32 [65536, 16], P(('region', 'sub')), may hold values from 0 to 1151, as said below
- degree: int32 [65536], P(('region', 'sub')), may hold values from 1 to 16
- send_rows: int32 [262144, 1], P(('region', 'sub')), may hold values from 0 to 127
- hub_rows: int32 [512], P(('region', 'sub')), may hold values from 0 to 127
Outputs:
- output: bfloat16 [65536, 1024], P(('region', 'sub'))
- grad_feat: bfloat16 [65536, 1024], P(('region', 'sub'))
Inputs may be any that keep to these rules, and one draw needn't show every extreme that they name: `nbr_index`: slots k >= degree[t] are padding and carry no edge.
All inputs are finite; a program needn't handle non-finite values.
Results may differ from a plain program's by a relative error of at most 0.0052.
Values may be sent and summed in bfloat16 or wider, within the bound.
A program may use at most 64 MiB of HBM per device.

v0:
```python
import jax
import jax.numpy as jnp
from jax import lax
from jax.sharding import PartitionSpec as P


def silu_slope(pre_act):
    sigmoid_value = jax.nn.sigmoid(pre_act)
    return sigmoid_value * (1.0 + pre_act * (1.0 - sigmoid_value))


def on_device(feat, cotangent, weight, nbr_index, degree, send_rows, hub_rows):
    node_count, feat_width = feat.shape
    region_count = lax.axis_size("region")
    sub_count = lax.axis_size("sub")
    bound_rows = send_rows.shape[1]
    slot_count = nbr_index.shape[1]
    outgoing = feat[send_rows.reshape(-1)].reshape(region_count, sub_count, bound_rows, feat_width)
    incoming = lax.all_to_all(
        lax.all_to_all(outgoing, "region", split_axis=0, concat_axis=0, tiled=True),
        "sub",
        split_axis=1,
        concat_axis=1,
        tiled=True,
    )
    hub_feat = lax.all_gather(feat[hub_rows], ("region", "sub"), axis=0, tiled=True)
    lookup = jnp.concatenate([feat, incoming.reshape(-1, feat_width), hub_feat], axis=0)
    lookup_rows = lookup.shape[0]

    def add_slot(slot_index, running):
        column = lax.dynamic_index_in_dim(nbr_index, slot_index, 1, keepdims=False)
        slot_live = slot_index < degree
        return running + jnp.where(slot_live[:, None], lookup[column].astype(jnp.float32), 0.0)

    summed = lax.fori_loop(0, slot_count, add_slot, feat.astype(jnp.float32))
    divisor = (degree + 1).astype(jnp.float32)[:, None]
    mean_rows = (summed / divisor).astype(jnp.bfloat16)
    full_weight = lax.all_gather(weight, "sub", axis=0, tiled=True)
    pre_act = jnp.dot(mean_rows, full_weight, preferred_element_type=jnp.float32)
    output_rows = jax.nn.silu(pre_act).astype(jnp.bfloat16)
    act_grad = (cotangent.astype(jnp.float32) * silu_slope(pre_act)).astype(jnp.bfloat16)
    back_proj = lax.dot_general(
        act_grad, full_weight, (((1,), (1,)), ((), ())), preferred_element_type=jnp.float32
    )
    per_target = back_proj / divisor

    def spread(slot_index, running):
        column = lax.dynamic_index_in_dim(nbr_index, slot_index, 1, keepdims=False)
        slot_live = slot_index < degree
        target = jnp.where(slot_live, column, lookup_rows)
        return running.at[target].add(per_target)

    grad_table = lax.fori_loop(
        0, slot_count, spread, jnp.zeros((lookup_rows + 1, feat_width), jnp.float32)
    )
    own_grad = grad_table[:node_count] + per_target
    bound_total = region_count * sub_count * bound_rows
    back_rows = grad_table[node_count : node_count + bound_total].reshape(
        region_count, sub_count, bound_rows, feat_width
    )
    returned = lax.all_to_all(
        lax.all_to_all(back_rows, "region", split_axis=0, concat_axis=0, tiled=True),
        "sub",
        split_axis=1,
        concat_axis=1,
        tiled=True,
    )
    own_grad = own_grad.at[send_rows.reshape(-1)].add(returned.reshape(-1, feat_width))
    hub_terms = grad_table[node_count + bound_total : lookup_rows]
    hub_grad = lax.psum_scatter(hub_terms, ("region", "sub"), scatter_dimension=0, tiled=True)
    own_grad = own_grad.at[hub_rows].add(hub_grad)
    return (output_rows, own_grad.astype(jnp.bfloat16))


def solution(mesh):
    placed = (
        P(("region", "sub"), None),
        P(("region", "sub"), None),
        P("sub", None),
        P(("region", "sub"), None),
        P(("region", "sub")),
        P(("region", "sub"), None),
        P(("region", "sub")),
    )
    return jax.shard_map(
        on_device,
        mesh=mesh,
        in_specs=placed,
        out_specs=(P(("region", "sub"), None), P(("region", "sub"), None)),
        check_vma=False,
    )
```

profile of v0, /device:TPU:1, one launch (start us, length us, event | category | flops | bytes accessed | tf_op | source)
XLA Modules:
  0.0 716.0 jit_solution(14145329363008141568)
XLA Ops:
  7.9 4.5 gather_fusion.1
  12.3 10.5 %all-to-all-start = ((bf16[16,32,1,1024]{3,1,2,0:T(8,128)(2,1)}), bf16[16,32,1,1024]{3,1,2,0:T(8,128)(2,1)S(1)}, u32[]{:S(2)}, u32[]{:S(2)}) async-start(bf16[16,32,1,1024]{3,1,2,0:T(8,128)(2,1)} %bitcast.5), calls=%async_computation | async-start | bytes 2097152 | tf_op jit(solution)/shard_map/all_to_all | solution.py:20
  24.1 26.6 %all-to-all-done = bf16[16,32,1,1024]{3,1,2,0:T(8,128)(2,1)S(1)} async-done(((bf16[16,32,1,1024]{3,1,2,0:T(8,128)(2,1)}), bf16[16,32,1,1024]{3,1,2,0:T(8,128)(2,1)S(1)}, u32[]{:S(2)}, u32[]{:S(2)}) %all-to-all-start) | async-done | bytes 1048608 | tf_op jit(solution)/shard_map/all_to_all | solution.py:20
  50.7 1.5 copy.14
  52.3 11.2 %all-to-all-start.1 = ((bf16[16,32,1,1024]{3,0,2,1:T(8,128)(2,1)}), bf16[16,32,1,1024]{3,0,2,1:T(8,128)(2,1)S(1)}, u32[]{:S(2)}, u32[]{:S(2)}) async-start(bf16[16,32,1,1024]{3,0,2,1:T(8,128)(2,1)} %copy.14), calls=%async_computation.1 | async-start | bytes 2097152 | tf_op jit(solution)/shard_map/all_to_all | solution.py:19
  64.3 84.3 %all-gather.6.cloned.1.call-done = bf16[512,1,1024]{2,1,0:T(2,128)(2,1)} async-done(((bf16[1,1,1024]{2,1,0:T(2,128)(2,1)}), bf16[512,1,1024]{2,1,0:T(2,128)(2,1)}) %all-gather.6.cloned.1.call-update) | async-done | bytes 1048592 | tf_op jit(solution)/shard_map/all_gather | solution.py:26
  148.6 3.0 copy.20
  153.0 28.4 %while.28 = (s32[]{:T(128)}, f32[128,1024]{1,0:T(8,128)S(1)}, s32[128]{0:T(128)S(1)}, s32[128,16]{0,1:T(8,128)}, bf16[1152,1024]{1,0:T(8,128)(2,1)S(1)}, /*index=5*/s32[]{:T(128)}) while((s32[]{:T(128)}, f32[128,1024]{1,0:T(8,128)S(1)}, s32[128]{0:T(128)S(1)}, s32[128,16]{0,1:T(8,128)}, bf16[1152,1024]{1,0:T(8,128)(2,1)S(1)}, ...), condition=%wide.region_1.2_spmd, body=%wide.region_0.1_spmd.sunk | while | flops 394754 | bytes 1842005 | solution.py:35
  153.0 0.7 fusion.11
  153.7 0.9 gather_fusion
  155.5 0.9 gather_fusion
  157.3 0.9 gather_fusion
  159.0 0.9 gather_fusion
  160.1 0.7 fusion.11
  160.8 0.9 gather_fusion
  161.9 0.7 fusion.11
  162.6 0.9 gather_fusion
  163.6 0.7 fusion.11
  164.4 0.9 gather_fusion
  165.4 0.7 fusion.11
  166.1 0.9 gather_fusion
  167.9 0.9 gather_fusion
  169.7 0.9 gather_fusion
  170.7 0.7 fusion.11
  171.4 0.9 gather_fusion
  173.2 0.9 gather_fusion
  175.0 0.9 gather_fusion
  176.8 0.9 gather_fusion
  177.8 0.7 fusion.11
  178.5 0.9 gather_fusion
  180.3 0.9 gather_fusion
  181.4 46.3 %all-gather.4.cloned.1.call-done = bf16[1024,1024]{1,0:T(8,128)(2,1)} async-done(((bf16[32,1024]{1,0:T(8,128)(2,1)}), bf16[1024,1024]{1,0:T(8,128)(2,1)}) %all-gather.4.cloned.1.call-update) | async-done | bytes 2097168 | tf_op jit(solution)/shard_map/all_gather | solution.py:38
  227.7 3.0 multiply_convert_fusion.1
  230.7 0.9 convolution_divide_fusion
  231.5 2.7 broadcast_in_dim.52
  234.2 107.6 %while.29 = (s32[]{:T(128)}, f32[1153,1024]{1,0:T(8,128)}, s32[128]{0:T(128)S(1)}, s32[128,16]{0,1:T(8,128)}, f32[128,1024]{1,0:T(8,128)S(1)}, /*index=5*/s32[]{:T(128)}) while((s32[]{:T(128)}, f32[1153,1024]{1,0:T(8,128)}, s32[128]{0:T(128)S(1)}, s32[128,16]{0,1:T(8,128)}, f32[128,1024]{1,0:T(8,128)S(1)}, /*index=5*/s32[]{:T(128)}) %tuple.80), condition=%wide.region_4.5_spmd, body=%wide.region_2.4_spmd.sunk | while | flops 131714 | bytes 1576013 | solution.py:53
  234.9 6.0 scatter_fusion
  241.7 6.0 scatter_fusion
  248.4 6.0 scatter_fusion
  255.1 6.0 scatter_fusion
  261.8 6.0 scatter_fusion
  268.6 6.0 scatter_fusion
  275.3 6.0 scatter_fusion
  282.0 6.0 scatter_fusion
  288.7 6.0 scatter_fusion
  295.5 6.0 scatter_fusion
  302.2 6.0 scatter_fusion
  308.9 6.0 scatter_fusion
  315.6 6.0 scatter_fusion
  322.4 6.0 scatter_fusion
  329.1 6.0 scatter_fusion
  335.8 6.0 scatter_fusion
  341.8 4.0 fusion.6
  345.9 62.2 %all_to_all.20 = f32[16,32,1,1024]{3,1,2,0:T(8,128)S(1)} all-to-all(f32[16,32,1,1024]{3,1,2,0:T(8,128)S(1)} %bitcast.32), channel_id=1, replica_groups=mesh['region'=16,'sub'=32] {'region'}, dimensions={0} | all-to-all | bytes 4194304 | tf_op jit(solution)/shard_map/all_to_all | solution.py:62
  408.1 2.6 copy.16
  410.7 5.5 all-to-all-start.3
  417.1 0.7 and_reduce_fusion
  417.8 1.1 slice_add_fusion
  418.9 49.3 %all-to-all-done.3 = f32[16,32,1,1024]{3,0,2,1:T(8,128)} async-done(((f32[16,32,1,1024]{3,0,2,1:T(8,128)}), f32[16,32,1,1024]{3,0,2,1:T(8,128)}, u32[]{:S(2)}, u32[]{:S(2)}) %all-to-all-start.3) | async-done | bytes 2097184 | tf_op jit(solution)/shard_map/all_to_all | solution.py:61
  468.2 2.8 copy.17
  471.1 5.1 scatter_fusion.1
  476.1 231.1 %all-reduce.3.cloned.1.call-done = f32[512,1024]{1,0:T(8,128)} async-done(((f32[512,1024]{1,0:T(8,128)}), f32[512,1024]{1,0:T(8,128)}) %all-reduce.3.cloned.1.call-update) | async-done | bytes 2097168
  707.2 1.4 broadcast_select_fusion
  708.7 0.7 convert_element_type.34
  (100 shorter events, 24.8 us)
Async XLA Ops:
  12.3 11.2 %copy-start = (bf16[128,1024]{1,0:T(8,128)(2,1)S(1)}, bf16[128,1024]{1,0:T(8,128)(2,1)}, u32[]{:S(2)}) copy-start(bf16[128,1024]{1,0:T(8,128)(2,1)} %param.13) | copy-start | bytes 786436
  12.3 38.4 %all-to-all-start = ((bf16[16,32,1,1024]{3,1,2,0:T(8,128)(2,1)}), bf16[16,32,1,1024]{3,1,2,0:T(8,128)(2,1)S(1)}, u32[]{:S(2)}, u32[]{:S(2)}) async-start(bf16[16,32,1,1024]{3,1,2,0:T(8,128)(2,1)} %bitcast.5), calls=%async_computation | async-start | bytes 2097152 | tf_op jit(solution)/shard_map/all_to_all | solution.py:20
  22.8 125.8 %all-gather.6.cloned.1.call-start = ((), (), s32[]{:S(2)}) async-start(), calls=%async_computation.5 | async-start | bytes 2101248 | tf_op jit(solution)/shard_map/all_gather | solution.py:26
  24.1 40.1 %copy-start.2 = (s32[128]{0:T(128)S(1)}, s32[128]{0:T(128)}, u32[]{:S(2)}) copy-start(s32[128]{0:T(128)} %param.17) | copy-start | bytes 1540
  52.3 99.3 %all-to-all-start.1 = ((bf16[16,32,1,1024]{3,0,2,1:T(8,128)(2,1)}), bf16[16,32,1,1024]{3,0,2,1:T(8,128)(2,1)S(1)}, u32[]{:S(2)}, u32[]{:S(2)}) async-start(bf16[16,32,1,1024]{3,0,2,1:T(8,128)(2,1)} %copy.14), calls=%async_computation.1 | async-start | bytes 2097152 | tf_op jit(solution)/shard_map/all_to_all | solution.py:19
  63.4 164.2 %all-gather.4.cloned.1.call-start = ((), (), s32[]{:S(2)}) async-start(), calls=%async_computation.4 | async-start | bytes 2162688 | tf_op jit(solution)/shard_map/all_gather | solution.py:38
  151.6 1.2 copy-start.1
  227.7 3.0 copy-start.4
  227.7 3.0 copy-start.5
  410.7 57.5 %all-to-all-start.3 = ((f32[16,32,1,1024]{3,0,2,1:T(8,128)}), f32[16,32,1,1024]{3,0,2,1:T(8,128)}, u32[]{:S(2)}, u32[]{:S(2)}) async-start(f32[16,32,1,1024]{3,0,2,1:T(8,128)} %copy.16), calls=%async_computation.3 | async-start | bytes 4194304 | tf_op jit(solution)/shard_map/all_to_all | solution.py:61
  416.3 0.8 copy-start.3
  416.3 290.9 %all-reduce.3.cloned.1.call-start = ((), (), s32[]{:S(2)}) async-start(), calls=%async_computation.6 | async-start | bytes 4194304
Sparse Core Ops, SparseCore 0:
  28.4 120.1 all-gather.5
  151.8 75.8 all-gather.3
  422.1 285.0 all-reduce.2
where the time goes:
time: 718 us; the launch traced here: 716 us
  waiting for transfers between devices  439 us (61%)
  other arithmetic  132 us (18%)
  blocking collectives  62.2 us (9%)
  local copies, waits for them, and re-layouts  36.9 us (5%)
  starting transfers between devices  27.3 us (4%)
  between operations  14.5 us (2%)
    unnamed x4, waiting for transfers between devices  232 us
    scatter-add x16, other arithmetic, spread(): return running.at[target].add(per_target)  96.5 us
    all_gather x1, waiting for transfers between devices, on_device(): lax.all_gather(feat[hub_rows], ('region', 'sub'), axis=0, tiled=True)  84.3 us
    all_to_all x1, blocking collectives, on_device(): lax.all_to_all(back_rows, 'region', split_axis=0, concat_axis=0, tiled=True)  62.2 us
    all_to_all x1, waiting for transfers between devices, on_device(): lax.all_to_all(lax.all_to_all(back_rows, 'region', split_axis=0, concat_a...  49.3 us
    all_gather x1, waiting for transfers between devices, on_device(): full_weight = lax.all_gather(weight, 'sub', axis=0, tiled=True)  46.3 us
    all_to_all x1, waiting for transfers between devices, on_device(): lax.all_to_all(outgoing, 'region', split_axis=0, concat_axis=0, tiled=True)  26.6 us
  transfers between devices with their start and end apart: 6, of which 5 were waited for; matrix products, arithmetic and copies ran while one was open for 6% of the time, Pallas kernels for 0%

commit v1 on v0

v1 whole, which is shorter than its diff:
```python
import jax
import jax.numpy as jnp
from jax import lax
from jax.experimental import pallas as pl
from jax.experimental.pallas import tpu as pltpu
from jax.sharding import PartitionSpec as P

MESH = pl.DeviceIdType.MESH
Y, X, Z = 8, 4, 8
CHIPS = Y * X * Z


def place():
    region = lax.axis_index("region")
    sub = lax.axis_index("sub")
    return region // 2, region % 2, sub // 8, sub % 8


def swap_kernel(send, recv, send_sem, recv_sem):
    y, core, x, z = place()
    chip = y * 32 + x * 8 + z

    def post(step, carry):
        mixed = (step * 77) % 256
        ty, tx, tz = (y + mixed // 32) % 8, (x + (mixed // 8) % 4) % 4, (z + mixed % 8) % 8
        pltpu.make_async_remote_copy(
            src_ref=send.at[ty * 32 + tx * 8 + tz],
            dst_ref=recv.at[chip],
            send_sem=send_sem,
            recv_sem=recv_sem,
            device_id=(ty * 2 + core, tx * 8 + tz),
            device_id_type=MESH,
        ).start()
        return carry

    lax.fori_loop(1, CHIPS, post, 0)
    most = pl.ds(0, CHIPS - 1)
    pltpu.make_async_copy(recv.at[most], recv.at[most], recv_sem).wait()
    pltpu.make_async_copy(send.at[most], send.at[most], send_sem).wait()
    recv[chip] = send[chip]


def swap(tiles):
    return pl.pallas_call(
        swap_kernel,
        out_shape=jax.ShapeDtypeStruct(tiles.shape, tiles.dtype),
        in_specs=[pl.BlockSpec(memory_space=pltpu.VMEM)],
        out_specs=pl.BlockSpec(memory_space=pltpu.VMEM),
        scratch_shapes=[pltpu.SemaphoreType.DMA, pltpu.SemaphoreType.DMA],
        compiler_params=pltpu.CompilerParams(has_side_effects=True, vmem_limit_bytes=32 << 20),
        name="swap",
    )(tiles)


def exchange(rows):
    core = lax.axis_index("region") % 2
    width = rows.shape[-1]
    tiles = rows.reshape(2, Y, 2, X * Z, width).transpose(1, 3, 2, 0, 4).reshape(CHIPS, 32, 128)
    came = swap(tiles).reshape(CHIPS, 2, 2, width)
    mine = lax.dynamic_index_in_dim(came, core, 1, keepdims=False)
    other = lax.dynamic_index_in_dim(came, 1 - core, 1, keepdims=False)
    pairs = [(r, r ^ 1) for r in range(16)]
    other = lax.ppermute(other, "region", pairs)
    first = jnp.where(core == 0, mine, other)
    second = jnp.where(core == 0, other, mine)
    both = jnp.stack([first, second], axis=1)
    return both.reshape(Y, X * Z, 2, 2, width).transpose(3, 0, 2, 1, 4).reshape(2, 512, width)


def silu_slope(pre_act):
    sigmoid_value = jax.nn.sigmoid(pre_act)
    return sigmoid_value * (1.0 + pre_act * (1.0 - sigmoid_value))


def on_device(feat, cotangent, weight, nbr_index, degree, send_rows, hub_rows):
    node_count, feat_width = feat.shape
    full_weight = lax.all_gather(weight, "sub", axis=0, tiled=True)
    own = jnp.arange(node_count, dtype=jnp.int32)
    picks = (send_rows == own[None, :]).astype(jnp.bfloat16)
    bound_out = jnp.dot(picks, feat, preferred_element_type=jnp.float32).astype(jnp.bfloat16)
    hub_out = jnp.broadcast_to(feat[hub_rows], bound_out.shape)
    incoming = exchange(jnp.stack([bound_out, hub_out]))
    lookup = jnp.concatenate([feat, incoming[0], incoming[1]], axis=0)
    columns = jnp.arange(lookup.shape[0], dtype=jnp.int32)
    slots = jnp.arange(nbr_index.shape[1], dtype=jnp.int32)
    live = jnp.where(slots[None, :] < degree[:, None], nbr_index, -1)
    counts = jnp.sum((live[:, :, None] == columns[None, None, :]).astype(jnp.float32), axis=1)
    edges = counts.astype(jnp.bfloat16)
    summed = feat.astype(jnp.float32) + jnp.dot(edges, lookup, preferred_element_type=jnp.float32)
    divisor = (degree + 1).astype(jnp.float32)[:, None]
    mean_rows = (summed / divisor).astype(jnp.bfloat16)
    pre_act = jnp.dot(mean_rows, full_weight, preferred_element_type=jnp.float32)
    output_rows = jax.nn.silu(pre_act).astype(jnp.bfloat16)
    act_grad = (cotangent.astype(jnp.float32) * silu_slope(pre_act)).astype(jnp.bfloat16)
    back_proj = lax.dot_general(
        act_grad, full_weight, (((1,), (1,)), ((), ())), preferred_element_type=jnp.float32
    )
    per_target = back_proj / divisor
    table = lax.dot_general(
        counts, per_target, (((0,), (0,)), ((), ())), precision=lax.Precision.HIGHEST, preferred_element_type=jnp.float32
    )
    own_grad = table[:node_count] + per_target
    outgoing = table[node_count:].astype(jnp.bfloat16).reshape(2, 512, feat_width)
    returned = exchange(outgoing)
    own_grad = own_grad + lax.dot_general(
        picks, returned[0], (((0,), (0,)), ((), ())), preferred_element_type=jnp.float32
    )
    hub_grad = jnp.sum(returned[1].astype(jnp.float32), axis=0)
    own_grad = own_grad + jnp.where((own == hub_rows[0])[:, None], hub_grad[None, :], 0.0)
    return (output_rows, own_grad.astype(jnp.bfloat16))


def solution(mesh):
    placed = (
        P(("region", "sub"), None),
        P(("region", "sub"), None),
        P("sub", None),
        P(("region", "sub"), None),
        P(("region", "sub")),
        P(("region", "sub"), None),
        P(("region", "sub")),
    )
    return jax.shard_map(
        on_device,
        mesh=mesh,
        in_specs=placed,
        out_specs=(P(("region", "sub"), None), P(("region", "sub"), None)),
        check_vma=False,
    )
```

time: 718 us -> 243 us (0.34)
  waiting for transfers between devices: 439 us -> 22.5 us
  Pallas kernels: 0 us -> 146 us
  other arithmetic: 132 us -> 9.18 us
  blocking collectives: 62.2 us -> 0 us
  starting transfers between devices: 27.3 us -> 6.85 us
  matrix products: 3.85 us -> 13.6 us
  local copies, waits for them, and re-layouts: 36.9 us -> 28.5 us
    unnamed x4 -> x1, waiting for transfers between devices: 232 us -> 0.68 us
    pallas_call x0 -> x2, Pallas kernels: none -> 146 us  [swap(): pl.pallas_call(swap_kernel, out_shape=jax.ShapeDtypeStruct(tiles.shape, t...]
    scatter-add x17 -> x0, other arithmetic: 102 us -> none  [the longest x16 96.5 us: spread(): return running.at[target].add(per_target)]
    all_gather x1 -> x0, waiting for transfers between devices: 84.3 us -> none  [on_device(): lax.all_gather(feat[hub_rows], ('region', 'sub'), axis=0, tiled=True)]
    all_to_all x3 -> x0, waiting for transfers between devices: 75.9 us -> none  [the longest x1 49.3 us: on_device(): lax.all_to_all(lax.all_to_all(back_rows, 'region', split_axis=0, concat_a...]
    all_to_all x1 -> x0, blocking collectives: 62.2 us -> none  [on_device(): lax.all_to_all(back_rows, 'region', split_axis=0, concat_axis=0, tiled=True)]
    all_to_all x3 -> x0, starting transfers between devices: 27.1 us -> none  [the longest x1 11.2 us: on_device(): lax.all_to_all(lax.all_to_all(outgoing, 'region', split_axis=0, concat_ax...]
    all_gather x1, waiting for transfers between devices: 46.3 us -> 19.6 us  [on_device(): full_weight = lax.all_gather(weight, 'sub', axis=0, tiled=True)]
  transfers between devices with their start and end apart: 6 -> 3, of which waited for: 5 -> 2; matrix products, arithmetic and copies ran while one was open for 6% -> 9% of each run, Pallas kernels for 0% -> 31%
where the time goes in v1:
time: 243 us; the launch traced here: 242 us
  Pallas kernels  146 us (60%)
  local copies, waits for them, and re-layouts  28.5 us (12%)
  waiting for transfers between devices  22.5 us (9%)
  between operations  15 us (6%)
  matrix products  13.6 us (6%)
  other arithmetic  9.18 us (4%)
  starting transfers between devices  6.85 us (3%)
    pallas_call x2, Pallas kernels, swap(): pl.pallas_call(swap_kernel, out_shape=jax.ShapeDtypeStruct(tiles.shape, t...  146 us
    all_gather x1, waiting for transfers between devices, on_device(): full_weight = lax.all_gather(weight, 'sub', axis=0, tiled=True)  19.6 us
    ppermute x2, starting transfers between devices, exchange(): other = lax.ppermute(other, 'region', pairs)  6.81 us
    unnamed x18, local copies, waits for them, and re-layouts  6.79 us
    reshape x2, local copies, waits for them, and re-layouts, exchange(): rows.reshape(2, Y, 2, X * Z, width).transpose(1, 3, 2, 0, 4)  6.3 us
    transpose x1, other arithmetic, exchange(): rows.reshape(2, Y, 2, X * Z, width).transpose(1, 3, 2, 0, 4)  5.62 us
    reshape x2, local copies, waits for them, and re-layouts, exchange(): came = swap(tiles).reshape(CHIPS, 2, 2, width)  5.09 us
  transfers between devices with their start and end apart: 3, of which 2 were waited for; matrix products, arithmetic and copies ran while one was open for 9% of the time, Pallas kernels for 31%

profile of v1, /device:TPU:1, one launch (start us, length us, event | category | flops | bytes accessed | tf_op | source)
XLA Modules:
  0.0 241.8 jit_solution(6290945036547816420)
XLA Ops:
  7.2 0.0 all-gather.2.cloned.1.call-start
  7.2 0.7 all-gather.2.cloned.1.call-update
  8.6 0.0 copy-start.3
  8.6 1.5 convolution_convert_fusion
  10.1 1.8 copy.27
  11.8 0.0 copy-done.3
  11.9 1.4 stack_broadcast_in_dim.2
  13.3 5.6 %maximum_bitcast_fusion = bf16[8,32,2,2,1024]{4,3,2,1,0:T(2,128)(2,1)} fusion(bf16[1,8,2,32,1024]{4,0,2,3,1:T(2,128)(2,1)S(1)} %stack_broadcast_in_dim.2, bf16[1,8,2,32,1024]{4,0,2,3,1:T(2,128)(2,1)S(1)} %copy.27), kind=kLoop, calls=%fused_computation.9 | loop fusion | flops 4194304 | bytes 4194304 | tf_op jit(solution)/shard_map/transpose | solution.py:58
  18.9 3.2 %reshape.51.send = bf16[256,32,128]{2,1,0:T(8,128)(2,1)S(1)} reshape(bf16[8,32,2,2,1024]{4,3,2,1,0:T(2,128)(2,1)} %maximum_bitcast_fusion) | data formatting | bytes 4194304 | tf_op jit(solution)/shard_map/reshape | solution.py:58
  22.1 75.4 %swap.2 = bf16[256,32,128]{2,1,0:T(8,128)(2,1)S(1)} custom-call(bf16[256,32,128]{2,1,0:T(8,128)(2,1)S(1)} %reshape.51.send), custom_call_target="tpu_custom_call" | custom-call | tf_op jit(solution)/shard_map/swap/pallas_call | solution.py:44
  97.5 0.0 copy-start
  97.5 1.3 copy-done
  98.8 2.5 %reshape.52 = bf16[256,2,2,1024]{3,2,1,0:T(2,128)(2,1)S(1)} reshape(bf16[256,32,128]{2,1,0:T(8,128)(2,1)} %copy-done) | data formatting | bytes 4194304 | tf_op jit(solution)/shard_map/reshape | solution.py:59
  101.4 1.4 constant_dynamic-slice_fusion.3
  102.8 0.0 copy-start.5
  102.9 0.0 copy-start.6
  102.9 1.3 copy.56
  104.1 3.5 %collective-permute-start = (bf16[256,2,1024]{2,0,1:T(8,128)(2,1)}, bf16[256,2,1024]{2,0,1:T(8,128)(2,1)S(1)}, u32[]{:S(2)}, u32[]{:S(2)}) collective-permute-start(bf16[256,2,1024]{2,0,1:T(8,128)(2,1)} %bitcast.52), channel_id=1, source_target_pairs={{0,32},{32,0},{64,96},{96,64},{128,160},{160,128},{192,224},{224,1... | collective-permute-start | bytes 3145736 | tf_op jit(solution)/shard_map/ppermute | solution.py:63
  107.6 0.0 copy-done.5
  107.6 0.0 copy-done.6
  107.7 0.1 copy.26
  107.8 2.2 convert_reduce_fusion
  110.0 0.0 collective-permute-done
  110.0 0.4 broadcast_select_fusion.3
  110.4 0.2 maximum_bitcast_fusion.1
  110.6 0.2 fusion.31
  110.8 19.6 %all-gather.2.cloned.1.call-done = bf16[1024,1024]{1,0:T(8,128)(2,1)} async-done(((bf16[32,1024]{1,0:T(8,128)(2,1)}), bf16[1024,1024]{1,0:T(8,128)(2,1)}) %all-gather.2.cloned.1.call-update) | async-done | bytes 2097168 | tf_op jit(solution)/shard_map/all_gather | solution.py:77
  130.4 0.0 copy-start.7
  130.4 3.4 %multiply_convert_fusion.1 = (bf16[128,1024]{1,0:T(8,128)(2,1)}, f32[128,1024]{1,0:T(8,128)}) fusion(bf16[1024,1024]{1,0:T(8,128)(2,1)} %all-gather.2.cloned.1.call-done, bf16[512,1024]{1,0:T(8,128)(2,1)S(1)} %bitcast.64, bf16[512,1024]{1,0:T(8,128)(2,1)S(1)} %bitcast.63, bf16[128,1024]{1,0:T(8,128)(2,1)S(1)} %copy-done.3, ...), kind=kOutput, calls=%fused_computation.33 | convolution fusion | flops 578830336 | bytes 5833216 | tf_op jit(solution)/shard_map/dot_general | solution.py:92
  133.8 0.0 copy-done.7
  133.8 2.6 %convolution_divide_fusion = f32[128,1024]{1,0:T(8,128)S(1)} fusion(bf16[1024,1024]{1,0:T(8,128)(2,1)} %all-gather.2.cloned.1.call-done, f32[128,1024]{1,0:T(8,128)} %get-tuple-element.24, bf16[128,1024]{1,0:T(8,128)(2,1)S(1)} %copy-done.7, f32[128]{0:T(128)S(1)} %add_convert_fusion), kind=kOutput, calls=%fused_computation.17 | convolution fusion | flops 269877248 | bytes 3408384 | tf_op jit(solution)/shard_map/dot_general | solution.py:95
  136.4 3.9 %fusion.36 = f32[1152,1024]{1,0:T(8,128)S(1)} fusion(f32[128,1152]{1,0:T(8,128)S(1)} %convert_reduce_fusion, f32[128,1024]{1,0:T(8,128)S(1)} %convolution_divide_fusion), kind=kOutput, calls=%fused_computation.54 | convolution fusion | flops 1811939328 | bytes 5832704 | tf_op jit(solution)/shard_map/dot_general | solution.py:99
  140.2 0.0 copy-start.2
  140.3 2.1 copy-done.2
  142.4 0.3 slice.47
  142.7 3.5 %copy.54 = bf16[2,8,2,32,1024]{4,0,2,3,1:T(2,128)(2,1)} copy(bf16[2,8,2,32,1024]{4,3,2,1,0:T(8,128)(2,1)S(1)} %bitcast.55) | data formatting | bytes 4194304 | tf_op jit(solution)/shard_map/reshape;reshape | solution.py:58
  146.3 3.2 %reshape.53.send = bf16[256,32,128]{2,1,0:T(8,128)(2,1)S(1)} reshape(bf16[8,32,2,2,1024]{4,3,2,1,0:T(2,128)(2,1)} %bitcast.54) | data formatting | bytes 4194304 | tf_op jit(solution)/shard_map/reshape | solution.py:58
  149.4 70.8 %swap.3 = bf16[256,32,128]{2,1,0:T(8,128)(2,1)S(1)} custom-call(bf16[256,32,128]{2,1,0:T(8,128)(2,1)S(1)} %reshape.53.send), custom_call_target="tpu_custom_call" | custom-call | tf_op jit(solution)/shard_map/swap/pallas_call | solution.py:44
  220.2 0.0 copy-start.1
  220.2 1.4 copy-done.1
  221.6 2.5 %reshape.54 = bf16[256,2,2,1024]{3,2,1,0:T(2,128)(2,1)S(1)} reshape(bf16[256,32,128]{2,1,0:T(8,128)(2,1)} %copy-done.1) | data formatting | bytes 4194304 | tf_op jit(solution)/shard_map/reshape | solution.py:59
  224.1 1.4 constant_dynamic-slice_fusion.1
  225.6 0.3 copy.55
  225.8 3.3 %collective-permute-start.1 = (bf16[256,2,1024]{2,0,1:T(8,128)(2,1)S(1)}, bf16[256,2,1024]{2,0,1:T(8,128)(2,1)S(1)}, u32[]{:S(2)}, u32[]{:S(2)}) collective-permute-start(bf16[256,2,1024]{2,0,1:T(8,128)(2,1)S(1)} %bitcast.62), channel_id=1, source_target_pairs={{0,32},{32,0},{64,96},{96,64},{128,160},{160,128},{192,224},{224,1... | collective-permute-start | bytes 3145736 | tf_op jit(solution)/shard_map/ppermute | solution.py:63
  229.2 2.3 collective-permute-done.1
  231.4 0.4 broadcast_select_fusion.1
  231.8 0.2 maximum_bitcast_fusion.2
  232.0 0.0 copy-start.4
  232.0 0.2 convert_reduce_fusion.1
  232.2 0.1 slice.40
  232.3 0.4 copy-done.4
  232.7 2.2 fusion.10
  (4 shorter events, 0.0 us)
Async XLA Ops:
  7.2 123.2 %all-gather.2.cloned.1.call-start = ((), (), s32[]{:S(2)}) async-start(), calls=%async_computation | async-start | bytes 2162688 | tf_op jit(solution)/shard_map/all_gather | solution.py:77
  8.6 3.3 %copy-start.3 = (bf16[128,1024]{1,0:T(8,128)(2,1)S(1)}, bf16[128,1024]{1,0:T(8,128)(2,1)}, u32[]{:S(2)}) copy-start(bf16[128,1024]{1,0:T(8,128)(2,1)} %param.7) | copy-start | bytes 786436
  97.5 1.3 copy-start
  102.8 4.8 %copy-start.5 = (s32[128,16]{0,1:T(8,128)S(1)}, s32[128,16]{0,1:T(8,128)}, u32[]{:S(2)}) copy-start(s32[128,16]{0,1:T(8,128)} %param.10) | copy-start | bytes 24580
  102.9 4.8 %copy-start.6 = (s32[128]{0:T(128)S(1)}, s32[128]{0:T(128)}, u32[]{:S(2)}) copy-start(s32[128]{0:T(128)} %param.11) | copy-start | bytes 1540
  104.1 5.9 %collective-permute-start = (bf16[256,2,1024]{2,0,1:T(8,128)(2,1)}, bf16[256,2,1024]{2,0,1:T(8,128)(2,1)S(1)}, u32[]{:S(2)}, u32[]{:S(2)}) collective-permute-start(bf16[256,2,1024]{2,0,1:T(8,128)(2,1)} %bitcast.52), channel_id=1, source_target_pairs={{0,32},{32,0},{64,96},{96,64},{128,160},{160,128},{192,224},{224,1... | collective-permute-start | bytes 3145736 | tf_op jit(solution)/shard_map/ppermute | solution.py:63
  130.4 3.4 %copy-start.7 = (bf16[128,1024]{1,0:T(8,128)(2,1)S(1)}, bf16[128,1024]{1,0:T(8,128)(2,1)}, u32[]{:S(2)}) copy-start(bf16[128,1024]{1,0:T(8,128)(2,1)} %param.8) | copy-start | bytes 786436
  140.2 2.1 copy-start.2
  220.2 1.4 copy-start.1
  225.8 5.6 %collective-permute-start.1 = (bf16[256,2,1024]{2,0,1:T(8,128)(2,1)S(1)}, bf16[256,2,1024]{2,0,1:T(8,128)(2,1)S(1)}, u32[]{:S(2)}, u32[]{:S(2)}) collective-permute-start(bf16[256,2,1024]{2,0,1:T(8,128)(2,1)S(1)} %bitcast.62), channel_id=1, source_target_pairs={{0,32},{32,0},{64,96},{96,64},{128,160},{160,128},{192,224},{224,1... | collective-permute-start | bytes 3145736 | tf_op jit(solution)/shard_map/ppermute | solution.py:63
  232.0 0.7 copy-start.4
Sparse Core Ops, SparseCore 0:
  11.2 119.1 all-gather.1

commit v2 on v0

v2 whole, which is shorter than its diff:
```python
import functools

import jax
import jax.numpy as jnp
from jax import lax
from jax.experimental import pallas as pl
from jax.experimental.pallas import tpu as pltpu
from jax.sharding import PartitionSpec as P

MESH = pl.DeviceIdType.MESH
BF16, F32 = jnp.bfloat16, jnp.float32
Y, X, Z = 8, 4, 8
CHIPS = Y * X * Z
NODES, WIDTH, BOUND, HUBS = 128, 1024, 512, 512
COLUMNS = NODES + BOUND + HUBS
CHUNKS = 4
PAIRS = CHIPS // 2 // CHUNKS


def place():
    region = lax.axis_index("region")
    sub = lax.axis_index("sub")
    return region // 2, region % 2, sub // 8, sub % 8


def device(y, core, x, z):
    return (y * 2 + core, x * 8 + z)


def remote(src, dst, send_sem, recv_sem, target):
    copy = pltpu.make_async_remote_copy(
        src_ref=src, dst_ref=dst, send_sem=send_sem, recv_sem=recv_sem, device_id=target, device_id_type=MESH
    )
    copy.start()


def await_bytes(ref, sem):
    pltpu.make_async_copy(ref, ref, sem).wait()


def dot(a, b):
    return jnp.dot(a, b, preferred_element_type=F32)


def whole_kernel(
    feat, cot, shard, live, divisor, send_row, hub_at,
    out, grad,
    picks_t, wide, full_weight, lookup, edges, edges_t, picks, pre, terms, high, low, own_sum,
    swap_out_f, swap_in_f, post_f, came_f, swap_out_b, swap_in_b, post_b, came_b,
    hub_tile, hub_other, hub_tiles, table, hub_table,
    hub_core, hub_x_out, hub_x_in, hub_x_sum, hub_y_out, hub_y_in, hub_y_sum, hub_z_in, hub_z_sum, hub_last, hub_row,
    swap_recv_f, swap_recv_b, send_sems, recv_sems,
):
    y, core, x, z = place()
    chip = y * 32 + x * 8 + z
    partner = device(y, 1 - core, x, z)
    holds = core == z // 4

    sem_ids = iter(range(32))

    def sems():
        i = next(sem_ids)
        return send_sems.at[i], recv_sems.at[i]

    def target_of(step):
        dz = step % 8
        dy = (step // 8 + step) % 8
        dx = step // 64
        return (y + dy) % 8, (x + dx) % 4, (z + dz) % 8

    def chip_of(at):
        return at[0] * 32 + at[1] * 8 + at[2]

    w_z, w_x, w_core = sems(), sems(), sems()
    half = pl.ds(pl.multiple_of(core * 16, 16), 16)
    for d in range(1, Z):
        remote(shard.at[half], full_weight.at[x, z, core], *w_z, device(y, core, x, (z + d) % 8))
    full_weight[x, z, 0] = shard[0:16]
    full_weight[x, z, 1] = shard[16:32]

    own_id = lax.broadcasted_iota(jnp.int32, (NODES, BOUND), 0)
    one_hot = jnp.where(own_id == send_row[...], 1.0, 0.0)
    picks[...] = one_hot.astype(BF16)
    for b in range(BOUND // 128):
        picks_t[b * 128 : (b + 1) * 128, :] = one_hot[:, b * 128 : (b + 1) * 128].T.astype(BF16)

    def in_tiles(ref, n, part):
        for e in range(2):
            ref[pl.ds(2 * n + e, 512, stride=8), :] = part[:, e * 128 : (e + 1) * 128]

    h_core, h_z, h_y, h_x, h_last = sems(), sems(), sems(), sems(), sems()
    hub_pick = jnp.where(lax.broadcasted_iota(jnp.int32, (16, NODES), 1) == hub_at[0], 1.0, 0.0).astype(BF16)
    hub_wide = dot(hub_pick, feat[...])[0:8]
    lane_group = lax.broadcasted_iota(jnp.int32, (8, 128), 0)
    own_hub = jnp.zeros((8, 128), F32)
    for j in range(8):
        own_hub = jnp.where(lane_group == j, hub_wide[:, j * 128 : (j + 1) * 128], own_hub)
    hub_tile[...] = jnp.concatenate([own_hub, own_hub], axis=0).astype(BF16)
    remote(hub_tile, hub_other, *h_core, partner)

    def swap_start(row, swap_out, swap_in, send_sem, recv_sem):
        for chunk in range(CHUNKS):

            def build(m, carry):
                first = row(chip_of(target_of(2 * m)), 1)
                second = row(chip_of(target_of(2 * m + 1)), 1)
                swap_out[m] = jnp.concatenate([first, second], axis=0).astype(BF16)
                return carry

            lax.fori_loop(chunk * PAIRS, (chunk + 1) * PAIRS, build, 0, unroll=4)
            part = pl.ds(chunk * PAIRS, PAIRS)
            remote(swap_out.at[part], swap_in.at[part], send_sem, recv_sem.at[chunk], partner)

    def post_chunk(chunk, row, swap_in, post, came, swap_recv, send_sem, recv_sem):
        await_bytes(swap_in.at[pl.ds(chunk * PAIRS, PAIRS)], swap_recv.at[chunk])

        def step(m, carry):
            other = swap_in[m].astype(F32)
            for e in range(2):
                i = 2 * m + e
                at = target_of(i)
                tile = jnp.concatenate([row(chip_of(at), 0), other[8 * e : 8 * e + 8]], axis=0).astype(BF16)
                post[i] = tile

                def go():
                    remote(post.at[i], came.at[chip], send_sem, recv_sem, device(at[0], core, at[1], at[2]))

                if e:
                    go()
                else:
                    pl.when(i > 0)(go)
            return carry

        lax.fori_loop(chunk * PAIRS, (chunk + 1) * PAIRS, step, 0)

    def exchange_end(post, came, swap_out, swap_send, send_sem, recv_sem):
        most = pl.ds(0, CHIPS - 1)
        await_bytes(came.at[most], recv_sem)
        came[chip] = post[0]

    def finish_sends(post, swap_out, swap_send, send_sem):
        await_bytes(post.at[pl.ds(0, CHIPS - 1)], send_sem)
        await_bytes(swap_out, swap_send)

    def to_rows(tiles, base):
        for part in range(8):
            wide[part * 512 : (part + 1) * 512, :] = tiles[part * 32 : (part + 1) * 32].reshape(512, 128).astype(F32)
        for j in range(8):
            lookup[base : base + 512, j * 128 : (j + 1) * 128] = wide[pl.ds(j, 512, stride=8), :].astype(BF16)

    bound_f, bound_b, swap_f, swap_b = sems(), sems(), sems(), sems()

    for n in range(4):
        in_tiles(table, n, dot(picks_t[...], feat[:, n * 256 : (n + 1) * 256]))

    def table_row(to_chip, other):
        return table[pl.ds(pl.multiple_of((to_chip * 2 + other) * 8, 8), 8), :]

    swap_start(table_row, swap_out_f, swap_in_f, swap_f[0], swap_recv_f)

    await_bytes(hub_other, h_core[1])
    theirs = hub_other[...].astype(F32)[0:8]
    first = jnp.where(core == 0, own_hub, theirs)
    second = jnp.where(core == 0, theirs, own_hub)
    z_slab = ((x * 2 + core) * 8 + y) * 4

    @pl.when(holds)
    def _():
        slot = z_slab + z % 4
        hub_tiles[slot] = jnp.concatenate([first, second], axis=0).astype(BF16)
        for d in range(1, Z):
            remote(hub_tiles.at[slot], hub_tiles.at[slot], *h_z, device(y, core, x, (z + d) % 8))

    forward = functools.partial(
        post_chunk, row=table_row, swap_in=swap_in_f, post=post_f, came=came_f, swap_recv=swap_recv_f,
        send_sem=bound_f[0], recv_sem=bound_f[1],
    )
    forward(0)

    await_bytes(full_weight.at[0, pl.ds(0, 7), 0], w_z[1])
    for d in range(1, X):
        to = (x + d) % 4
        remote(full_weight.at[x, :, core], full_weight.at[x, :, core], *w_x, device(y, core, to, z))

    @pl.when(holds)
    def _():
        await_bytes(hub_tiles.at[pl.ds(0, 3)], h_z[1])
        await_bytes(hub_tiles.at[pl.ds(0, 7)], h_z[0])

    @pl.when(jnp.logical_not(holds))
    def _():
        await_bytes(hub_tiles.at[pl.ds(0, 4)], h_z[1])

    y_slab = pl.ds(z_slab, 4)
    for d in range(1, Y):
        remote(hub_tiles.at[y_slab], hub_tiles.at[y_slab], *h_y, device((y + d) % 8, core, x, z))
    forward(1)

    await_bytes(hub_tiles.at[pl.ds(0, 28)], h_y[1])
    x_slab = pl.ds((x * 2 + core) * 32, 32)
    for d in range(1, X):
        remote(hub_tiles.at[x_slab], hub_tiles.at[x_slab], *h_x, device(y, core, (x + d) % 4, z))
    forward(2)
    forward(3)

    await_bytes(full_weight.at[pl.ds(0, 3), :, 0], w_x[1])
    remote(full_weight.at[:, :, core], full_weight.at[:, :, core], *w_core, partner)
    await_bytes(hub_tiles.at[pl.ds(0, 96)], h_x[1])
    for at in range(X):
        slab = pl.ds((at * 2 + core) * 32, 32)
        remote(hub_tiles.at[slab], hub_tiles.at[slab], *h_last, partner)

    for b in range(COLUMNS // 128):
        row_id = lax.broadcasted_iota(jnp.int32, (128, 128), 0) + b * 128
        count = jnp.zeros((128, 128), F32)
        for k in range(live.shape[0]):
            count = count + jnp.where(live[k : k + 1, :] == row_id, 1.0, 0.0)
        edges_t[b * 128 : (b + 1) * 128, :] = count.astype(BF16)
        edges[:, b * 128 : (b + 1) * 128] = count.T.astype(BF16)
    lookup[0:NODES, :] = feat[...]
    await_bytes(hub_tiles.at[pl.ds(0, 128)], h_last[1])
    to_rows(hub_tiles, NODES + BOUND)
    await_bytes(full_weight.at[:, :, 0], w_core[1])
    exchange_end(post_f, came_f, swap_out_f, swap_f[0], *bound_f)
    to_rows(came_f, NODES)

    div = divisor[...]
    for n in range(4):
        cols = slice(n * 256, (n + 1) * 256)
        summed = feat[:, cols].astype(F32) + dot(edges[...], lookup[:, cols])
        high[:, cols] = (summed / div).astype(BF16)
    for n in range(4):
        cols = slice(n * 256, (n + 1) * 256)
        total = jnp.zeros((NODES, 256), F32)
        for k in range(X):
            total = total + dot(high[:, k * 256 : (k + 1) * 256], full_weight[k, :, :, :, cols].reshape(256, 256))
        sig = jax.nn.sigmoid(total)
        out[:, cols] = (total * sig).astype(BF16)
        slope = sig * (1.0 + total * (1.0 - sig))
        pre[:, cols] = (cot[:, cols].astype(F32) * slope).astype(BF16)
    for n in range(X):
        cols = slice(n * 256, (n + 1) * 256)
        term = lax.dot_general(
            pre[...], full_weight[n].reshape(256, WIDTH), (((1,), (1,)), ((), ())), preferred_element_type=F32
        ) / div
        top = term.astype(BF16)
        terms[:, cols] = term
        high[:, cols] = top
        low[:, cols] = (term - top.astype(F32)).astype(BF16)

    def spread(rows, ref):
        for n in range(4):
            cols = slice(n * 256, (n + 1) * 256)
            in_tiles(ref, n, dot(edges_t[rows, :], high[:, cols]) + dot(edges_t[rows, :], low[:, cols]))

    g_core, g_x, g_y, g_z, g_last = sems(), sems(), sems(), sems(), sems()
    spread(slice(NODES + BOUND, COLUMNS), hub_table)
    for at in range(X):
        slab = pl.ds(pl.multiple_of((at * 2 + 1 - core) * 512, 512), 512)
        remote(hub_table.at[slab], hub_core.at[at], *g_core, partner)

    spread(slice(NODES, NODES + BOUND), table)

    swap_start(table_row, swap_out_b, swap_in_b, swap_b[0], swap_recv_b)
    backward = functools.partial(
        post_chunk, row=table_row, swap_in=swap_in_b, post=post_b, came=came_b, swap_recv=swap_recv_b,
        send_sem=bound_b[0], recv_sem=bound_b[1],
    )

    def kept(at):
        return hub_table[pl.ds(pl.multiple_of((at * 2 + core) * 512, 512), 512), :] + hub_core[at]

    await_bytes(hub_core, g_core[1])
    for d in range(1, X):
        to = (x + d) % 4
        hub_x_out[d - 1] = kept(to).astype(BF16)
        remote(hub_x_out.at[d - 1], hub_x_in.at[d - 1], *g_x, device(y, core, to, z))
    backward(0)
    backward(1)

    await_bytes(hub_x_in, g_x[1])
    part = kept(x)
    for d in range(X - 1):
        part = part + hub_x_in[d].astype(F32)
    hub_x_sum[...] = part
    hub_y_out[...] = part.astype(BF16).reshape(Y, 64, 128)
    for d in range(1, Y):
        to = (y + d) % 8
        remote(hub_y_out.at[to], hub_y_in.at[d - 1], *g_y, device(to, core, x, z))
    backward(2)

    await_bytes(hub_y_in, g_y[1])
    part = hub_x_sum[pl.ds(pl.multiple_of(y * 64, 64), 64), :]
    for d in range(Y - 1):
        part = part + hub_y_in[d].astype(F32)
    hub_y_sum[...] = part
    for at in range(4):
        to = core * 4 + at

        @pl.when(to != z)
        def _():
            slot = (to - z + 8) % 8 - 1
            remote(hub_y_sum.at[pl.ds(at * 16, 16)], hub_z_in.at[slot], *g_z, device(y, core, x, to))

    backward(3)

    @pl.when(holds)
    def _():
        await_bytes(hub_z_in, g_z[1])
        total = hub_y_sum[pl.ds(pl.multiple_of((z % 4) * 16, 16), 16), :]
        for d in range(Z - 1):
            total = total + hub_z_in[d]
        hub_z_sum[...] = total
        remote(hub_z_sum, hub_last, *g_last, partner)
        hub_row[...] = hub_z_sum[pl.ds(pl.multiple_of(core * 8, 8), 8), :]
        await_bytes(hub_z_in.at[pl.ds(0, 3)], g_z[0])
        await_bytes(hub_z_sum, g_last[0])

    @pl.when(jnp.logical_not(holds))
    def _():
        await_bytes(hub_last, g_last[1])
        hub_row[...] = hub_last[pl.ds(pl.multiple_of(core * 8, 8), 8), :]
        await_bytes(hub_z_in.at[pl.ds(0, 4)], g_z[0])

    hub_mask = lax.broadcasted_iota(jnp.int32, (NODES, 128), 0) == hub_at[0]
    for n in range(4):
        cols = slice(n * 256, (n + 1) * 256)
        own_sum[:, cols] = (
            terms[:, cols] + dot(edges_t[0:NODES, :], high[:, cols]) + dot(edges_t[0:NODES, :], low[:, cols])
        )
    for j in range(8):
        cols = slice(j * 128, (j + 1) * 128)
        own_sum[:, cols] += jnp.where(hub_mask, hub_row[j : j + 1, :], 0.0)
    exchange_end(post_b, came_b, swap_out_b, swap_b[0], *bound_b)
    to_rows(came_b, NODES)
    for n in range(4):
        cols = slice(n * 256, (n + 1) * 256)
        grad[:, cols] = (own_sum[:, cols] + dot(picks[...], lookup[NODES : NODES + BOUND, cols])).astype(BF16)

    for d in range(1, Z):
        await_bytes(shard.at[half], w_z[0])
    await_bytes(full_weight.at[pl.ds(0, 3), :, 0], w_x[0])
    await_bytes(full_weight.at[:, :, 0], w_core[0])
    await_bytes(hub_tile, h_core[0])
    await_bytes(hub_tiles.at[pl.ds(0, 28)], h_y[0])
    await_bytes(hub_tiles.at[pl.ds(0, 96)], h_x[0])
    await_bytes(hub_tiles.at[pl.ds(0, 128)], h_last[0])
    await_bytes(hub_core, g_core[0])
    await_bytes(hub_x_in, g_x[0])
    await_bytes(hub_y_in, g_y[0])
    finish_sends(post_f, swap_out_f, swap_f[0], bound_f[0])
    finish_sends(post_b, swap_out_b, swap_b[0], bound_b[0])


def tiles(count):
    return pltpu.VMEM((count, 16, 128), BF16)


SCRATCH = [
    pltpu.VMEM((BOUND, NODES), BF16),
    pltpu.VMEM((4096, 128), F32),
    pltpu.VMEM((X, Z, 2, 16, WIDTH), BF16),
    pltpu.VMEM((COLUMNS, WIDTH), BF16),
    pltpu.VMEM((NODES, COLUMNS), BF16),
    pltpu.VMEM((COLUMNS, NODES), BF16),
    pltpu.VMEM((NODES, BOUND), BF16),
    pltpu.VMEM((NODES, WIDTH), BF16),
    pltpu.VMEM((NODES, WIDTH), F32),
    pltpu.VMEM((NODES, WIDTH), BF16),
    pltpu.VMEM((NODES, WIDTH), BF16),
    pltpu.VMEM((NODES, WIDTH), F32),
    tiles(128), tiles(128), tiles(256), tiles(256),
    tiles(128), tiles(128), tiles(256), tiles(256),
    pltpu.VMEM((16, 128), BF16),
    pltpu.VMEM((16, 128), BF16),
    tiles(256),
    pltpu.VMEM((4096, 128), F32),
    pltpu.VMEM((4096, 128), F32),
    pltpu.VMEM((X, 512, 128), F32),
    pltpu.VMEM((X - 1, 512, 128), BF16),
    pltpu.VMEM((X - 1, 512, 128), BF16),
    pltpu.VMEM((512, 128), F32),
    pltpu.VMEM((Y, 64, 128), BF16),
    pltpu.VMEM((Y - 1, 64, 128), BF16),
    pltpu.VMEM((64, 128), F32),
    pltpu.VMEM((Z - 1, 16, 128), F32),
    pltpu.VMEM((16, 128), F32),
    pltpu.VMEM((16, 128), F32),
    pltpu.VMEM((8, 128), F32),
    pltpu.SemaphoreType.DMA((CHUNKS,)),
    pltpu.SemaphoreType.DMA((CHUNKS,)),
    pltpu.SemaphoreType.DMA((20,)),
    pltpu.SemaphoreType.DMA((20,)),
]


def on_device(feat, cotangent, weight, nbr_index, degree, send_rows, hub_rows):
    core = lax.axis_index("region") % 2
    s = nbr_index - NODES
    bound_column = NODES + ((s // 64) * 32 + s % 32) * 2 + ((s // 32) % 2 + core) % 2
    h = nbr_index - (NODES + BOUND)
    hub_column = (
        NODES + BOUND
        + ((((h % 32) // 8 * 2 + (h % 8) // 4) * 8 + h // 64) * 4 + h % 4) * 2
        + (h // 32) % 2
    )
    column = jnp.where(
        nbr_index < NODES, nbr_index, jnp.where(nbr_index < NODES + BOUND, bound_column, hub_column)
    )
    slots = jnp.arange(nbr_index.shape[1], dtype=jnp.int32)
    live = jnp.where(slots[None, :] < degree[:, None], column, -1).T
    divisor = (degree + 1).astype(F32)[:, None]
    by_core = send_rows.reshape(Y, 2, 32)
    by_core = jnp.where(core == 0, by_core, by_core[:, ::-1])
    send_at = by_core.transpose(0, 2, 1).reshape(BOUND)
    vmem = pl.BlockSpec(memory_space=pltpu.VMEM)
    smem = pl.BlockSpec(memory_space=pltpu.SMEM)
    return pl.pallas_call(
        whole_kernel,
        out_shape=(
            jax.ShapeDtypeStruct((NODES, WIDTH), BF16),
            jax.ShapeDtypeStruct((NODES, WIDTH), BF16),
        ),
        in_specs=[vmem] * 6 + [smem],
        out_specs=(vmem, vmem),
        scratch_shapes=SCRATCH,
        compiler_params=pltpu.CompilerParams(has_side_effects=True, vmem_limit_bytes=48 << 20),
        name="sage",
    )(feat, cotangent, weight, live, divisor, send_at[None, :], hub_rows)


def solution(mesh):
    placed = (
        P(("region", "sub"), None),
        P(("region", "sub"), None),
        P("sub", None),
        P(("region", "sub"), None),
        P(("region", "sub")),
        P(("region", "sub"), None),
        P(("region", "sub")),
    )
    return jax.shard_map(
        on_device,
        mesh=mesh,
        in_specs=placed,
        out_specs=(P(("region", "sub"), None), P(("region", "sub"), None)),
        check_vma=False,
    )
```

time: 718 us -> 114 us (0.16)
  waiting for transfers between devices: 439 us -> 0 us
  other arithmetic: 132 us -> 0.75 us
  Pallas kernels: 0 us -> 108 us
  blocking collectives: 62.2 us -> 0 us
  local copies, waits for them, and re-layouts: 36.9 us -> 3.48 us
  starting transfers between devices: 27.3 us -> 0 us
  between operations: 14.5 us -> 1.39 us
    unnamed x4 -> x0, waiting for transfers between devices: 232 us -> none
    all_gather x2 -> x0, waiting for transfers between devices: 131 us -> none  [the longest x1 84.3 us: on_device(): lax.all_gather(feat[hub_rows], ('region', 'sub'), axis=0, tiled=True)]
    pallas_call x0 -> x1, Pallas kernels: none -> 108 us  [on_device(): pl.pallas_call(whole_kernel, out_shape=(jax.ShapeDtypeStruct((NODES, WIDT...]
    scatter-add x17 -> x0, other arithmetic: 102 us -> none  [the longest x16 96.5 us: spread(): return running.at[target].add(per_target)]
    all_to_all x3 -> x0, waiting for transfers between devices: 75.9 us -> none  [the longest x1 49.3 us: on_device(): lax.all_to_all(lax.all_to_all(back_rows, 'region', split_axis=0, concat_a...]
    all_to_all x1 -> x0, blocking collectives: 62.2 us -> none  [on_device(): lax.all_to_all(back_rows, 'region', split_axis=0, concat_axis=0, tiled=True)]
    all_to_all x3 -> x0, starting transfers between devices: 27.1 us -> none  [the longest x1 11.2 us: on_device(): lax.all_to_all(lax.all_to_all(outgoing, 'region', split_axis=0, concat_ax...]
    select_n x33 -> x0, other arithmetic: 23 us -> none  [the longest x16 11.2 us: add_slot(): lookup[column].astype(jnp.float32)]
  transfers between devices with their start and end apart: 6 -> 0, of which waited for: 5 -> 0; matrix products, arithmetic and copies ran while one was open for 6% -> 0% of each run, Pallas kernels for 0% -> 0%
where the time goes in v2:
time: 114 us
  Pallas kernels  108 us (95%)
  local copies, waits for them, and re-layouts  3.48 us (3%)
  between operations  1.39 us (1%)
    pallas_call x1, Pallas kernels, on_device(): pl.pallas_call(whole_kernel, out_shape=(jax.ShapeDtypeStruct((NODES, WIDT...  108 us
    unnamed x15, local copies, waits for them, and re-layouts  2.93 us

profile of v2, /device:TPU:1, one launch (start us, length us, event | category | flops | bytes accessed | tf_op | source)
XLA Modules:
  0.0 114.0 jit_solution(15118129717978786907)
XLA Ops:
  0.6 0.0 copy-start.5
  1.3 0.0 copy-done.5
  1.3 0.0 copy-start.4
  1.3 0.0 copy-start.3
  1.4 0.5 broadcast.90
  1.9 0.1 copy-done.4
  2.0 0.7 reduce.3
  2.7 0.1 reshape.8
  2.8 0.0 copy-done.3
  2.8 0.1 select_bitcast_fusion.1.live
  2.8 0.1 copy.14.divisor
  2.9 0.1 copy.13
  3.1 0.0 copy-start.2
  3.1 0.1 rev.3
  3.2 0.0 copy-start
  3.2 0.0 copy-start.1
  3.2 0.1 broadcast_in_dim_reshape.3.send_row
  3.4 0.5 copy-done.2
  3.9 0.2 copy-done
  4.1 0.1 copy-done.1
  4.2 108.4 %sage.1 = (bf16[128,1024]{1,0:T(8,128)(2,1)S(1)}, bf16[128,1024]{1,0:T(8,128)(2,1)S(1)}) custom-call(bf16[128,1024]{1,0:T(8,128)(2,1)S(1)} %copy-done, bf16[128,1024]{1,0:T(8,128)(2,1)S(1)} %copy-done.1, bf16[32,1024]{1,0:T(8,128)(2,1)S(1)} %copy-done.2, s32[16,128]{1,0:T(8,128)S(1)} %select_bitcast_fusion.1.live, f32[128,1]{1,0:T(8,128)S(1)} %copy.14.divisor, ...), custom_call_target="tpu_custom_call" | custom-call | tf_op jit(solution)/shard_map/sage/pallas_call | solution.py:418
  112.6 0.7 copy.18
  113.3 0.7 copy.19
  (2 shorter events, 0.0 us)
Async XLA Ops:
  0.6 0.7 copy-start.5
  1.3 0.7 copy-start.4
  1.3 1.4 %copy-start.3 = (s32[128,16]{0,1:T(8,128)S(1)}, s32[128,16]{0,1:T(8,128)}, u32[]{:S(2)}) copy-start(s32[128,16]{0,1:T(8,128)} %param.10) | copy-start | bytes 24580
  3.1 0.8 copy-start.2
  3.2 1.0 copy-start
  3.2 1.0 copy-start.1

commit v3 on v0

v3 whole, which is shorter than its diff:
```python
import jax
import jax.numpy as jnp
from jax import lax
from jax.experimental import pallas as pl
from jax.experimental.pallas import tpu as pltpu
from jax.sharding import PartitionSpec as P

MESH = pl.DeviceIdType.MESH
BF16, F32, I32 = jnp.bfloat16, jnp.float32, jnp.int32
Y, X, Z = 8, 4, 8
CHIPS = Y * X * Z
PLANE = Y * Z
NODES, WIDTH, BOUND, HUBS = 128, 1024, 512, 512
COLUMNS = NODES + BOUND + HUBS
STEPS = (2, 1, 3, 0)


def place():
    region = lax.axis_index("region")
    sub = lax.axis_index("sub")
    return region // 2, region % 2, sub // 8, sub % 8


def device(y, core, x, z):
    return (y * 2 + core, x * 8 + z)


def remote(src, dst, sems, target):
    pltpu.make_async_remote_copy(
        src_ref=src, dst_ref=dst, send_sem=sems[0], recv_sem=sems[1], device_id=target, device_id_type=MESH
    ).start()


def await_bytes(ref, sem):
    pltpu.make_async_copy(ref, ref, sem).wait()


def dot(a, b):
    return jnp.dot(a, b, preferred_element_type=F32)


def block(n):
    return slice(n * 256, (n + 1) * 256)


def whole_kernel(
    feat, cot, shard, nbr_t, degree, send_row, hub_at,
    out, grad,
    pick_rows, picks, table, wide, full_weight, edges, edges_t, hub_lookup, div, total, mean, act, terms, high, low, own_sum,
    swap_out_f, swap_in_f, post_f, came_f, swap_out_b, swap_in_b, post_b, came_b,
    hub_tile, hub_other, hub_tiles, hub_table,
    hub_core, hub_x_out, hub_x_in, hub_x_sum, hub_y_out, hub_y_in, hub_y_sum, hub_z_in, hub_z_sum, hub_last, hub_row,
    send_sems, recv_sems, entered,
):
    y, core, x, z = place()
    chip = x * PLANE + y * 8 + z
    partner = device(y, 1 - core, x, z)
    holds = core == z // 4
    sem_ids = iter(range(64))
    due = {}
    sent = []

    def sems():
        i = next(sem_ids)
        return send_sems.at[i], recv_sems.at[i]

    def expect(name, ref, sem):
        due[name] = lambda: await_bytes(ref, sem)

    def settle(name):
        due.pop(name)()

    def leaves(ref, sem):
        sent.append(lambda: await_bytes(ref, sem))

    barrier = pltpu.get_barrier_semaphore()
    y_line = [device((y + d) % 8, core, x, z) for d in range(1, Y)]
    z_line = [device(y, core, x, (z + d) % 8) for d in range(1, Z)]
    x_line = [device(y, core, (x + d) % 4, z) for d in range(1, X)]
    for other in [partner] + x_line + y_line + z_line:
        pl.semaphore_signal(barrier, inc=1, device_id=other, device_id_type=MESH)

    own_id = lax.broadcasted_iota(I32, (NODES, 128), 0)
    for b in range(BOUND // 128):
        one_hot = jnp.where(own_id == send_row[:, b * 128 : (b + 1) * 128], 1.0, 0.0)
        pick_rows[b * 128 : (b + 1) * 128, :] = one_hot.T
    hub_pick = jnp.where(lax.broadcasted_iota(I32, (16, NODES), 1) == hub_at[0], 1.0, 0.0).astype(BF16)
    hub_wide = dot(hub_pick, feat[...])[0:8]
    lane_group = lax.broadcasted_iota(I32, (8, 128), 0)
    own_hub = jnp.zeros((8, 128), F32)
    for j in range(8):
        own_hub = jnp.where(lane_group == j, hub_wide[:, j * 128 : (j + 1) * 128], own_hub)
    hub_tile[...] = jnp.concatenate([own_hub, own_hub], axis=0).astype(BF16)
    pl.semaphore_wait(barrier, len(x_line) + len(y_line) + len(z_line) + 1)

    w_z, w_x, w_core = sems(), sems(), sems()
    half = pl.ds(pl.multiple_of(core * 16, 16), 16)
    for other in z_line:
        remote(shard.at[half], full_weight.at[x, z, core], w_z, other)
    expect("w_z", full_weight.at[0, pl.ds(0, 7), 0], w_z[1])
    leaves(full_weight.at[0, pl.ds(0, 7), 0], w_z[0])
    for other in y_line:
        pl.semaphore_signal(entered.at[0], inc=1, device_id=other, device_id_type=MESH)
    h_core, h_z, h_y, h_x, h_last = sems(), sems(), sems(), sems(), sems()
    remote(hub_tile, hub_other, h_core, partner)
    expect("h_core", hub_other, h_core[1])
    leaves(hub_tile, h_core[0])
    full_weight[x, z, 0] = shard[0:16]
    full_weight[x, z, 1] = shard[16:32]

    def in_tiles(ref, base, n, part):
        for e in range(2):
            ref[pl.ds(base + 2 * n + e, part.shape[0], stride=8), :] = part[:, e * 128 : (e + 1) * 128]

    def table_row(to, which):
        row = to[1] * 128 + which * 64 + to[0] * 8 + to[2]
        return table[pl.ds(pl.multiple_of(row * 8, 8), 8), :]

    def target_of(k, i):
        return (y + i // 8 + i) % 8, (x + STEPS[k]) % 4, (z + i) % 8

    def swap_start(k, swap_out, swap_in, pair):
        def build(m, carry):
            first = table_row(target_of(k, 2 * m), 1)
            second = table_row(target_of(k, 2 * m + 1), 1)
            swap_out[k * 32 + m] = jnp.concatenate([first, second], axis=0).astype(BF16)
            return carry

        lax.fori_loop(0, 32, build, 0, unroll=4)
        part = pl.ds(k * 32, 32)
        remote(swap_out.at[part], swap_in.at[part], pair, partner)
        expect(("swap", k), swap_in.at[part], pair[1])
        leaves(swap_out.at[part], pair[0])

    def post_quarter(k, swap_in, post, came, pair):
        settle(("swap", k))

        def step(m, carry):
            theirs = swap_in[k * 32 + m].astype(F32)
            for e in range(2):
                i = 2 * m + e
                to = target_of(k, i)
                tile = jnp.concatenate([table_row(to, 0), theirs[8 * e : 8 * e + 8]], axis=0).astype(BF16)
                at = k * 64 + i

                def go():
                    post[at] = tile
                    remote(post.at[at], came.at[chip], pair, device(to[0], core, to[1], to[2]))

                if e or STEPS[k]:
                    go()
                else:
                    pl.when(i > 0)(go)

                    @pl.when(i == 0)
                    def _():
                        came[chip] = tile
            return carry

        lax.fori_loop(0, 32, step, 0)
        count = 64 if STEPS[k] else 63
        expect(("came", k), came.at[pl.ds(0, count)], pair[1])
        leaves(post.at[pl.ds(0, count)], pair[0])

    def received(k, came):
        settle(("came", k))
        from_x = (x + 4 - STEPS[k]) % 4
        for part in range(4):
            wide[part * 256 : (part + 1) * 256, :] = (
                came[pl.ds(from_x * 64 + part * 16, 16)].reshape(256, 128).astype(F32)
            )

        def columns(n):
            sides = []
            for j in (2 * n, 2 * n + 1):
                sides.append(
                    jnp.concatenate([wide[pl.ds(w * 8 + j, 64, stride=16), :] for w in range(2)], axis=0)
                )
            return jnp.concatenate(sides, axis=1).astype(BF16)

        return from_x, columns

    swaps_f = [sems() for _ in STEPS]
    bounds_f = [sems() for _ in STEPS]

    def select(k):
        to_x = (x + STEPS[k]) % 4
        rows = []
        for which in range(2):
            other = (core + which) % 2
            for to_y in range(Y):
                rows.append(pick_rows[pl.ds(pl.multiple_of(to_y * 64 + other * 32 + to_x * 8, 8), 8), :])
        chosen = jnp.concatenate(rows, axis=0)
        picks[to_x] = chosen.T.astype(BF16)
        chosen = chosen.astype(BF16)
        for n in range(4):
            in_tiles(table, to_x * 1024, n, dot(chosen, feat[:, block(n)]))
        swap_start(k, swap_out_f, swap_in_f, swaps_f[k])

    select(0)

    settle("h_core")
    theirs = hub_other[...].astype(F32)[0:8]
    first = jnp.where(core == 0, own_hub, theirs)
    second = jnp.where(core == 0, theirs, own_hub)
    z_slab = ((x * 2 + core) * 8 + y) * 4

    @pl.when(holds)
    def _():
        slot = z_slab + z % 4
        hub_tiles[slot] = jnp.concatenate([first, second], axis=0).astype(BF16)
        for other in z_line:
            remote(hub_tiles.at[slot], hub_tiles.at[slot], h_z, other)

    def hub_z_due():
        @pl.when(holds)
        def _():
            await_bytes(hub_tiles.at[pl.ds(0, 3)], h_z[1])

        @pl.when(jnp.logical_not(holds))
        def _():
            await_bytes(hub_tiles.at[pl.ds(0, 4)], h_z[1])

    def hub_z_left():
        @pl.when(holds)
        def _():
            await_bytes(hub_tiles.at[pl.ds(0, 7)], h_z[0])

    due["h_z"] = hub_z_due
    sent.append(hub_z_left)
    pl.semaphore_wait(entered.at[0], Y - 1)
    for other in z_line:
        pl.semaphore_signal(entered.at[1], inc=1, device_id=other, device_id_type=MESH)
    select(1)
    pl.semaphore_wait(entered.at[1], Z - 1)
    post_quarter(0, swap_in_f, post_f, came_f, bounds_f[0])
    select(2)

    settle("w_z")
    for other in x_line:
        remote(full_weight.at[x, :, core], full_weight.at[x, :, core], w_x, other)
    expect("w_x", full_weight.at[pl.ds(0, 3), :, 0], w_x[1])
    leaves(full_weight.at[pl.ds(0, 3), :, 0], w_x[0])
    settle("h_z")
    y_slab = pl.ds(z_slab, 4)
    for other in y_line:
        remote(hub_tiles.at[y_slab], hub_tiles.at[y_slab], h_y, other)
    expect("h_y", hub_tiles.at[pl.ds(0, 28)], h_y[1])
    leaves(hub_tiles.at[pl.ds(0, 28)], h_y[0])
    post_quarter(1, swap_in_f, post_f, came_f, bounds_f[1])
    select(3)

    settle("h_y")
    x_slab = pl.ds((x * 2 + core) * 32, 32)
    for other in x_line:
        remote(hub_tiles.at[x_slab], hub_tiles.at[x_slab], h_x, other)
    expect("h_x", hub_tiles.at[pl.ds(0, 96)], h_x[1])
    leaves(hub_tiles.at[pl.ds(0, 96)], h_x[0])
    post_quarter(2, swap_in_f, post_f, came_f, bounds_f[2])
    post_quarter(3, swap_in_f, post_f, came_f, bounds_f[3])

    settle("h_x")
    for at in range(X):
        slab = pl.ds((at * 2 + core) * 32, 32)
        remote(hub_tiles.at[slab], hub_tiles.at[slab], h_last, partner)
    expect("h_last", hub_tiles.at[pl.ds(0, 128)], h_last[1])
    leaves(hub_tiles.at[pl.ds(0, 128)], h_last[0])
    settle("w_x")
    remote(full_weight.at[:, :, core], full_weight.at[:, :, core], w_core, partner)
    expect("w_core", full_weight.at[:, :, 0], w_core[1])
    leaves(full_weight.at[:, :, 0], w_core[0])

    number = nbr_t[...]
    s = number - NODES
    bound_column = (
        NODES + ((s >> 3) & 3) * 128 + (((s >> 5) + core) & 1) * 64 + (s >> 6) * 8 + (s & 7)
    )
    h = number - (NODES + BOUND)
    hub_column = (
        NODES + BOUND
        + ((((h >> 3) & 3) * 2 + ((h >> 2) & 1)) * 32 + (h >> 6) * 4 + (h & 3)) * 2
        + ((h >> 5) & 1)
    )
    column = jnp.where(number < NODES, number, jnp.where(number < NODES + BOUND, bound_column, hub_column))
    slot_id = lax.broadcasted_iota(I32, number.shape, 0)
    live = jnp.where(slot_id < degree[...], column, -1)
    for b in range(COLUMNS // 128):
        row_id = own_id + b * 128
        count = jnp.zeros((128, 128), F32)
        for k in range(live.shape[0]):
            count = count + jnp.where(live[k : k + 1, :] == row_id, 1.0, 0.0)
        edges_t[b * 128 : (b + 1) * 128, :] = count.astype(BF16)
        edges[:, b * 128 : (b + 1) * 128] = count.T.astype(BF16)
    div[...] = jnp.broadcast_to((degree[...] + 1).astype(F32), (128, 128)).T
    for n in range(4):
        rows = feat[:, block(n)]
        total[:, block(n)] = rows.astype(F32) + dot(edges[:, 0:NODES], rows)

    settle("h_last")
    for part in range(8):
        hub_table[part * 512 : (part + 1) * 512, :] = (
            hub_tiles[part * 32 : (part + 1) * 32].reshape(512, 128).astype(F32)
        )
    for j in range(8):
        hub_lookup[:, j * 128 : (j + 1) * 128] = hub_table[pl.ds(j, HUBS, stride=8), :].astype(BF16)
    for n in range(4):
        total[:, block(n)] += dot(edges[:, NODES + BOUND : COLUMNS], hub_lookup[:, block(n)])
    settle("w_core")

    for k in range(X):
        from_x, rows = received(k, came_f)
        part = edges[:, pl.ds(pl.multiple_of(NODES + from_x * 128, 128), 128)]
        for n in range(4):
            total[:, block(n)] += dot(part, rows(n))

    two_div = jnp.concatenate([div[...], div[...]], axis=1)
    for n in range(4):
        mean[:, block(n)] = (total[:, block(n)] / two_div).astype(BF16)
    for n in range(4):
        pre_act = jnp.zeros((NODES, 256), F32)
        for k in range(X):
            pre_act = pre_act + dot(mean[:, block(k)], full_weight[k, :, :, :, block(n)].reshape(256, 256))
        sig = jax.nn.sigmoid(pre_act)
        out[:, block(n)] = (pre_act * sig).astype(BF16)
        slope = sig * (1.0 + pre_act * (1.0 - sig))
        act[:, block(n)] = (cot[:, block(n)].astype(F32) * slope).astype(BF16)
    for n in range(X):
        term = lax.dot_general(
            act[...], full_weight[n].reshape(256, WIDTH), (((1,), (1,)), ((), ())), preferred_element_type=F32
        ) / two_div
        top = term.astype(BF16)
        terms[:, block(n)] = term
        high[:, block(n)] = top
        low[:, block(n)] = (term - top.astype(F32)).astype(BF16)

    def spread(rows, ref, base):
        edge = edges_t[rows, :]
        for n in range(4):
            in_tiles(ref, base, n, dot(edge, high[:, block(n)]) + dot(edge, low[:, block(n)]))

    swaps_b = [sems() for _ in STEPS]
    bounds_b = [sems() for _ in STEPS]
    g_core, g_x, g_y, g_z, g_last = sems(), sems(), sems(), sems(), sems()

    def give_back(k):
        to_x = (x + STEPS[k]) % 4
        spread(pl.ds(pl.multiple_of(NODES + to_x * 128, 128), 128), table, to_x * 1024)
        swap_start(k, swap_out_b, swap_in_b, swaps_b[k])

    give_back(0)

    spread(slice(NODES + BOUND, COLUMNS), hub_table, 0)
    for at in range(X):
        slab = pl.ds(pl.multiple_of((at * 2 + 1 - core) * 512, 512), 512)
        remote(hub_table.at[slab], hub_core.at[at], g_core, partner)
    expect("g_core", hub_core, g_core[1])
    leaves(hub_core, g_core[0])
    give_back(1)
    post_quarter(0, swap_in_b, post_b, came_b, bounds_b[0])

    def kept(at):
        return hub_table[pl.ds(pl.multiple_of((at * 2 + core) * 512, 512), 512), :] + hub_core[at]

    settle("g_core")
    for d in range(1, X):
        hub_x_out[d - 1] = kept((x + d) % 4).astype(BF16)
        remote(hub_x_out.at[d - 1], hub_x_in.at[d - 1], g_x, x_line[d - 1])
    expect("g_x", hub_x_in, g_x[1])
    leaves(hub_x_in, g_x[0])
    give_back(2)
    post_quarter(1, swap_in_b, post_b, came_b, bounds_b[1])
    give_back(3)

    settle("g_x")
    part = kept(x)
    for d in range(X - 1):
        part = part + hub_x_in[d].astype(F32)
    hub_x_sum[...] = part
    hub_y_out[...] = part.astype(BF16).reshape(Y, 64, 128)
    for d in range(1, Y):
        remote(hub_y_out.at[(y + d) % 8], hub_y_in.at[d - 1], g_y, y_line[d - 1])
    expect("g_y", hub_y_in, g_y[1])
    leaves(hub_y_in, g_y[0])
    post_quarter(2, swap_in_b, post_b, came_b, bounds_b[2])
    post_quarter(3, swap_in_b, post_b, came_b, bounds_b[3])

    for n in range(4):
        cols = block(n)
        own_sum[:, cols] = terms[:, cols] + dot(edges_t[0:NODES, :], high[:, cols]) + dot(edges_t[0:NODES, :], low[:, cols])
    settle("g_y")
    part = hub_x_sum[pl.ds(pl.multiple_of(y * 64, 64), 64), :]
    for d in range(Y - 1):
        part = part + hub_y_in[d].astype(F32)
    hub_y_sum[...] = part
    for at in range(4):
        to = core * 4 + at

        @pl.when(to != z)
        def _():
            slot = (to - z + 8) % 8 - 1
            remote(hub_y_sum.at[pl.ds(at * 16, 16)], hub_z_in.at[slot], g_z, device(y, core, x, to))

    for k in range(2):
        from_x, rows = received(k, came_b)
        for n in range(4):
            own_sum[:, block(n)] += dot(picks[from_x], rows(n))

    @pl.when(holds)
    def _():
        await_bytes(hub_z_in, g_z[1])
        here = hub_y_sum[pl.ds(pl.multiple_of((z % 4) * 16, 16), 16), :]
        for d in range(Z - 1):
            here = here + hub_z_in[d]
        hub_z_sum[...] = here
        remote(hub_z_sum, hub_last, g_last, partner)
        hub_row[...] = hub_z_sum[pl.ds(pl.multiple_of(core * 8, 8), 8), :]
        await_bytes(hub_z_in.at[pl.ds(0, 3)], g_z[0])
        await_bytes(hub_z_sum, g_last[0])

    @pl.when(jnp.logical_not(holds))
    def _():
        await_bytes(hub_last, g_last[1])
        hub_row[...] = hub_last[pl.ds(pl.multiple_of(core * 8, 8), 8), :]
        await_bytes(hub_z_in.at[pl.ds(0, 4)], g_z[0])

    hub_mask = own_id == hub_at[0]
    for j in range(8):
        cols = slice(j * 128, (j + 1) * 128)
        own_sum[:, cols] += jnp.where(hub_mask, hub_row[j : j + 1, :], 0.0)

    from_x, rows = received(2, came_b)
    for n in range(4):
        own_sum[:, block(n)] += dot(picks[from_x], rows(n))
    from_x, rows = received(3, came_b)
    for n in range(4):
        grad[:, block(n)] = (own_sum[:, block(n)] + dot(picks[from_x], rows(n))).astype(BF16)
    for wait in sent:
        wait()


def tiles(count):
    return pltpu.VMEM((count, 16, 128), BF16)


SCRATCH = [
    pltpu.VMEM((BOUND, NODES), F32),
    pltpu.VMEM((X, NODES, 128), BF16),
    pltpu.VMEM((4096, 128), F32),
    pltpu.VMEM((1024, 128), F32),
    pltpu.VMEM((X, Z, 2, 16, WIDTH), BF16),
    pltpu.VMEM((NODES, COLUMNS), BF16),
    pltpu.VMEM((COLUMNS, NODES), BF16),
    pltpu.VMEM((HUBS, WIDTH), BF16),
    pltpu.VMEM((128, 128), F32),
    pltpu.VMEM((NODES, WIDTH), F32),
    pltpu.VMEM((NODES, WIDTH), BF16),
    pltpu.VMEM((NODES, WIDTH), BF16),
    pltpu.VMEM((NODES, WIDTH), F32),
    pltpu.VMEM((NODES, WIDTH), BF16),
    pltpu.VMEM((NODES, WIDTH), BF16),
    pltpu.VMEM((NODES, WIDTH), F32),
    tiles(128), tiles(128), tiles(256), tiles(256),
    tiles(128), tiles(128), tiles(256), tiles(256),
    pltpu.VMEM((16, 128), BF16),
    pltpu.VMEM((16, 128), BF16),
    tiles(256),
    pltpu.VMEM((4096, 128), F32),
    pltpu.VMEM((X, 512, 128), F32),
    pltpu.VMEM((X - 1, 512, 128), BF16),
    pltpu.VMEM((X - 1, 512, 128), BF16),
    pltpu.VMEM((512, 128), F32),
    pltpu.VMEM((Y, 64, 128), BF16),
    pltpu.VMEM((Y - 1, 64, 128), BF16),
    pltpu.VMEM((64, 128), F32),
    pltpu.VMEM((Z - 1, 16, 128), F32),
    pltpu.VMEM((16, 128), F32),
    pltpu.VMEM((16, 128), F32),
    pltpu.VMEM((8, 128), F32),
    pltpu.SemaphoreType.DMA((32,)),
    pltpu.SemaphoreType.DMA((32,)),
    pltpu.SemaphoreType.REGULAR((2,)),
]


def on_device(feat, cotangent, weight, nbr_index, degree, send_rows, hub_rows):
    vmem = pl.BlockSpec(memory_space=pltpu.VMEM)
    smem = pl.BlockSpec(memory_space=pltpu.SMEM)
    return pl.pallas_call(
        whole_kernel,
        out_shape=(
            jax.ShapeDtypeStruct((NODES, WIDTH), BF16),
            jax.ShapeDtypeStruct((NODES, WIDTH), BF16),
        ),
        in_specs=[vmem] * 6 + [smem],
        out_specs=(vmem, vmem),
        scratch_shapes=SCRATCH,
        compiler_params=pltpu.CompilerParams(has_side_effects=True, collective_id=0, vmem_limit_bytes=48 << 20),
        name="sage",
    )(feat, cotangent, weight, nbr_index.T, degree[None, :], send_rows.T, hub_rows)


def solution(mesh):
    placed = (
        P(("region", "sub"), None),
        P(("region", "sub"), None),
        P("sub", None),
        P(("region", "sub"), None),
        P(("region", "sub")),
        P(("region", "sub"), None),
        P(("region", "sub")),
    )
    return jax.shard_map(
        on_device,
        mesh=mesh,
        in_specs=placed,
        out_specs=(P(("region", "sub"), None), P(("region", "sub"), None)),
        check_vma=False,
    )
```

time: 718 us -> 106 us (0.15)
  waiting for transfers between devices: 439 us -> 0 us
  other arithmetic: 132 us -> 0 us
  Pallas kernels: 0 us -> 99.1 us
  blocking collectives: 62.2 us -> 0 us
  local copies, waits for them, and re-layouts: 36.9 us -> 5.51 us
  starting transfers between devices: 27.3 us -> 0 us
  between operations: 14.5 us -> 1.31 us
    unnamed x4 -> x0, waiting for transfers between devices: 232 us -> none
    all_gather x2 -> x0, waiting for transfers between devices: 131 us -> none  [the longest x1 84.3 us: on_device(): lax.all_gather(feat[hub_rows], ('region', 'sub'), axis=0, tiled=True)]
    scatter-add x17 -> x0, other arithmetic: 102 us -> none  [the longest x16 96.5 us: spread(): return running.at[target].add(per_target)]
    pallas_call x0 -> x1, Pallas kernels: none -> 99.1 us  [on_device(): pl.pallas_call(whole_kernel, out_shape=(jax.ShapeDtypeStruct((NODES, WIDT...]
    all_to_all x3 -> x0, waiting for transfers between devices: 75.9 us -> none  [the longest x1 49.3 us: on_device(): lax.all_to_all(lax.all_to_all(back_rows, 'region', split_axis=0, concat_a...]
    all_to_all x1 -> x0, blocking collectives: 62.2 us -> none  [on_device(): lax.all_to_all(back_rows, 'region', split_axis=0, concat_axis=0, tiled=True)]
    all_to_all x3 -> x0, starting transfers between devices: 27.1 us -> none  [the longest x1 11.2 us: on_device(): lax.all_to_all(lax.all_to_all(outgoing, 'region', split_axis=0, concat_ax...]
    select_n x33 -> x0, other arithmetic: 23 us -> none  [the longest x16 11.2 us: add_slot(): lookup[column].astype(jnp.float32)]
  transfers between devices with their start and end apart: 6 -> 0, of which waited for: 5 -> 0; matrix products, arithmetic and copies ran while one was open for 6% -> 0% of each run, Pallas kernels for 0% -> 0%
where the time goes in v3:
time: 106 us
  Pallas kernels  99.1 us (93%)
  local copies, waits for them, and re-layouts  5.51 us (5%)
  between operations  1.31 us (1%)
    pallas_call x1, Pallas kernels, on_device(): pl.pallas_call(whole_kernel, out_shape=(jax.ShapeDtypeStruct((NODES, WIDT...  99.1 us
    unnamed x14, local copies, waits for them, and re-layouts  5.51 us

profile of v3, /device:TPU:1, one launch (start us, length us, event | category | flops | bytes accessed | tf_op | source)
XLA Modules:
  0.0 105.9 jit_solution(12300636419748577902)
XLA Ops:
  1.3 0.0 copy-start.4
  1.3 0.0 copy-start.5
  1.3 0.7 copy-done.4
  2.0 0.0 copy-done.5
  2.0 0.0 copy-start
  2.0 0.9 copy-done
  2.9 0.0 copy-start.1
  2.9 0.9 copy-done.1
  3.9 0.0 copy-start.2
  3.9 0.8 copy-done.2
  4.7 0.0 copy-start.3
  4.7 0.7 copy-done.3
  5.4 99.1 %sage.1 = (bf16[128,1024]{1,0:T(8,128)(2,1)S(1)}, bf16[128,1024]{1,0:T(8,128)(2,1)S(1)}) custom-call(bf16[128,1024]{1,0:T(8,128)(2,1)S(1)} %copy-done, bf16[128,1024]{1,0:T(8,128)(2,1)S(1)} %copy-done.1, bf16[32,1024]{1,0:T(8,128)(2,1)S(1)} %copy-done.2, s32[16,128]{1,0:T(8,128)S(1)} %bitcast.3, s32[1,128]{1,0:T(1,128)S(1)} %bitcast.5, ...), custom_call_target="tpu_custom_call" | custom-call | tf_op jit(solution)/shard_map/sage/pallas_call | solution.py:488
  104.5 0.7 copy.12
  105.2 0.7 copy.13
Async XLA Ops:
  1.3 0.7 copy-start.4
  1.3 0.7 copy-start.5
  2.0 1.0 copy-start
  2.9 0.9 copy-start.1
  3.9 0.8 copy-start.2
  4.7 0.7 copy-start.3

commit v4 on v3

--- a/solution.py
+++ b/solution.py
@@ -12,7 +12,7 @@
 PLANE = Y * Z
 NODES, WIDTH, BOUND, HUBS = 128, 1024, 512, 512
 COLUMNS = NODES + BOUND + HUBS
-STEPS = (2, 1, 3, 0)
+GROUPS = (2, 1, 3, 0)
 
 
 def place():
@@ -44,16 +44,17 @@
 
 
 def whole_kernel(
-    feat, cot, shard, nbr_t, degree, send_row, hub_at,
+    feat_hbm, cot_hbm, shard_hbm, nbr_hbm, degree_hbm, send_hbm, hub_at,
     out, grad,
+    feat, cot, shard, nbr_t, degree, send_row,
     pick_rows, picks, table, wide, full_weight, edges, edges_t, hub_lookup, div, total, mean, act, terms, high, low, own_sum,
-    swap_out_f, swap_in_f, post_f, came_f, swap_out_b, swap_in_b, post_b, came_b,
+    swap_out_f, swap_in_f, stage_f, mid_f, came_f, swap_out_b, swap_in_b, stage_b, mid_b, came_b,
     hub_tile, hub_other, hub_tiles, hub_table,
     hub_core, hub_x_out, hub_x_in, hub_x_sum, hub_y_out, hub_y_in, hub_y_sum, hub_z_in, hub_z_sum, hub_last, hub_row,
-    send_sems, recv_sems, entered,
+    send_sems, recv_sems, load_sems, entered,
 ):
     y, core, x, z = place()
-    chip = x * PLANE + y * 8 + z
+    slot_y = (y % 4) * 2 + y // 4
     partner = device(y, 1 - core, x, z)
     holds = core == z // 4
     sem_ids = iter(range(64))
@@ -80,17 +81,27 @@
     for other in [partner] + x_line + y_line + z_line:
         pl.semaphore_signal(barrier, inc=1, device_id=other, device_id_type=MESH)
 
+    loads = []
+    for i, (src, dst) in enumerate(
+        zip((send_hbm, feat_hbm, shard_hbm, nbr_hbm, degree_hbm, cot_hbm), (send_row, feat, shard, nbr_t, degree, cot))
+    ):
+        loads.append(pltpu.make_async_copy(src, dst, load_sems.at[i]))
+        loads[i].start()
+
+    loads[0].wait()
     own_id = lax.broadcasted_iota(I32, (NODES, 128), 0)
     for b in range(BOUND // 128):
         one_hot = jnp.where(own_id == send_row[:, b * 128 : (b + 1) * 128], 1.0, 0.0)
         pick_rows[b * 128 : (b + 1) * 128, :] = one_hot.T
     hub_pick = jnp.where(lax.broadcasted_iota(I32, (16, NODES), 1) == hub_at[0], 1.0, 0.0).astype(BF16)
+    loads[1].wait()
     hub_wide = dot(hub_pick, feat[...])[0:8]
     lane_group = lax.broadcasted_iota(I32, (8, 128), 0)
     own_hub = jnp.zeros((8, 128), F32)
     for j in range(8):
         own_hub = jnp.where(lane_group == j, hub_wide[:, j * 128 : (j + 1) * 128], own_hub)
     hub_tile[...] = jnp.concatenate([own_hub, own_hub], axis=0).astype(BF16)
+    loads[2].wait()
     pl.semaphore_wait(barrier, len(x_line) + len(y_line) + len(z_line) + 1)
 
     w_z, w_x, w_core = sems(), sems(), sems()
@@ -112,92 +123,123 @@
         for e in range(2):
             ref[pl.ds(base + 2 * n + e, part.shape[0], stride=8), :] = part[:, e * 128 : (e + 1) * 128]
 
-    def table_row(to, which):
-        row = to[1] * 128 + which * 64 + to[0] * 8 + to[2]
+    def table_row(g, dx, i, which):
+        row = ((y + g + i // 8 * 4) % 8) * 64 + which * 32 + (4 - dx) % 4 * 8 + (z + i) % 8
         return table[pl.ds(pl.multiple_of(row * 8, 8), 8), :]
 
-    def target_of(k, i):
-        return (y + i // 8 + i) % 8, (x + STEPS[k]) % 4, (z + i) % 8
-
-    def swap_start(k, swap_out, swap_in, pair):
-        def build(m, carry):
-            first = table_row(target_of(k, 2 * m), 1)
-            second = table_row(target_of(k, 2 * m + 1), 1)
-            swap_out[k * 32 + m] = jnp.concatenate([first, second], axis=0).astype(BF16)
+    def swap_start(g, ends):
+        swap_out, swap_in, pair = ends["swap_out"], ends["swap_in"], ends["swap"][g]
+        for dx in range(X):
+
+            def build(m, carry):
+                rows = [table_row(g, dx, 2 * m + e, 1) for e in range(2)]
+                swap_out[g * 32 + dx * 8 + m] = jnp.concatenate(rows, axis=0).astype(BF16)
+                return carry
+
+            lax.fori_loop(0, 8, build, 0, unroll=4)
+        part = pl.ds(g * 32, 32)
+        remote(swap_out.at[part], swap_in.at[part], pair, partner)
+        expect(("swap", g), swap_in.at[part], pair[1])
+        leaves(swap_out.at[part], pair[0])
+
+    def along_x(g, ends):
+        stage, mid = ends["stage"], ends["mid"]
+        settle(("swap", g))
+        for dx in (2, 1, 3, 0):
+
+            def pair_up(m, carry):
+                theirs = ends["swap_in"][g * 32 + dx * 8 + m].astype(F32)
+                for e in range(2):
+                    i = 2 * m + e
+                    tile = jnp.concatenate([table_row(g, dx, i, 0), theirs[8 * e : 8 * e + 8]], axis=0)
+                    stage[g, dx, i] = tile.astype(BF16)
+                return carry
+
+            lax.fori_loop(0, 8, pair_up, 0, unroll=4)
+            if dx:
+                remote(stage.at[g, dx], mid.at[g, dx - 1], ends["x"][g], x_line[dx - 1])
+        expect(("x", g), mid.at[g], ends["x"][g][1])
+        leaves(mid.at[g], ends["x"][g][0])
+
+    def to_plane(g, ends, name, src, dst, tile_count):
+        pair = ends[name][g]
+
+        def post(i, carry):
+            to = device((y + g + i // 8 * 4) % 8, core, x, (z + i) % 8)
+            remote(src(i), dst, pair, to)
             return carry
 
-        lax.fori_loop(0, 32, build, 0, unroll=4)
-        part = pl.ds(k * 32, 32)
-        remote(swap_out.at[part], swap_in.at[part], pair, partner)
-        expect(("swap", k), swap_in.at[part], pair[1])
-        leaves(swap_out.at[part], pair[0])
-
-    def post_quarter(k, swap_in, post, came, pair):
-        settle(("swap", k))
-
-        def step(m, carry):
-            theirs = swap_in[k * 32 + m].astype(F32)
-            for e in range(2):
-                i = 2 * m + e
-                to = target_of(k, i)
-                tile = jnp.concatenate([table_row(to, 0), theirs[8 * e : 8 * e + 8]], axis=0).astype(BF16)
-                at = k * 64 + i
-
-                def go():
-                    post[at] = tile
-                    remote(post.at[at], came.at[chip], pair, device(to[0], core, to[1], to[2]))
-
-                if e or STEPS[k]:
-                    go()
-                else:
-                    pl.when(i > 0)(go)
-
-                    @pl.when(i == 0)
-                    def _():
-                        came[chip] = tile
-            return carry
-
-        lax.fori_loop(0, 32, step, 0)
-        count = 64 if STEPS[k] else 63
-        expect(("came", k), came.at[pl.ds(0, count)], pair[1])
-        leaves(post.at[pl.ds(0, count)], pair[0])
-
-    def received(k, came):
-        settle(("came", k))
-        from_x = (x + 4 - STEPS[k]) % 4
-        for part in range(4):
-            wide[part * 256 : (part + 1) * 256, :] = (
-                came[pl.ds(from_x * 64 + part * 16, 16)].reshape(256, 128).astype(F32)
-            )
+        first = 0 if g else 1
+        lax.fori_loop(first, 16, post, 0)
+        same_size = tile_count(16 - first)
+        expect((name, g), same_size, pair[1])
+        leaves(same_size, pair[0])
+
+    def post_own(g, ends):
+        stage, came = ends["stage"], ends["came"]
+        to_plane(
+            g, ends, "own", lambda i: stage.at[g, 0, i], came.at[slot_y, 0, z], lambda n: stage.at[g, 0, pl.ds(0, n)]
+        )
+        if g == 0:
+            came[slot_y, 0, z] = stage[0, 0, 0]
+
+    def post_far(g, ends):
+        mid, came = ends["mid"], ends["came"]
+        settle(("x", g))
+        to_plane(
+            g, ends, "far", lambda i: mid.at[g, :, i], came.at[slot_y, pl.ds(1, 3), z], lambda n: mid.at[g, :, pl.ds(0, n)]
+        )
+        if g == 0:
+            for d in range(3):
+                came[slot_y, 1 + d, z] = mid[0, d, 0]
+
+    def received(g, ends):
+        came = ends["came"]
+        settle(("own", g))
+        settle(("far", g))
+        from_y = (y + 4 - g) % 4
+        for h in range(2):
+            wide[h * 512 : (h + 1) * 512, :] = came[from_y * 2 + h].reshape(512, 128).astype(F32)
 
         def columns(n):
             sides = []
             for j in (2 * n, 2 * n + 1):
-                sides.append(
-                    jnp.concatenate([wide[pl.ds(w * 8 + j, 64, stride=16), :] for w in range(2)], axis=0)
-                )
+                parts = [wide[pl.ds(h * 512 + w * 8 + j, 32, stride=16), :] for h in range(2) for w in range(2)]
+                sides.append(jnp.concatenate(parts, axis=0))
             return jnp.concatenate(sides, axis=1).astype(BF16)
 
-        return from_x, columns
-
-    swaps_f = [sems() for _ in STEPS]
-    bounds_f = [sems() for _ in STEPS]
-
-    def select(k):
-        to_x = (x + STEPS[k]) % 4
+        return from_y, columns
+
+    def exchange_ends(swap_out, swap_in, stage, mid, came):
+        ends = dict(swap_out=swap_out, swap_in=swap_in, stage=stage, mid=mid, came=came)
+        for name in ("swap", "x", "own", "far"):
+            ends[name] = [sems() for _ in GROUPS]
+        return ends
+
+    def to_table(base_y, n, part):
+        for h in range(2):
+            in_tiles(table, (h * 4 + base_y) * 512, n, part[h * 64 : (h + 1) * 64])
+
+    ends_f = exchange_ends(swap_out_f, swap_in_f, stage_f, mid_f, came_f)
+
+    def select(g):
+        to_y = (y + g) % 4
         rows = []
-        for which in range(2):
-            other = (core + which) % 2
-            for to_y in range(Y):
-                rows.append(pick_rows[pl.ds(pl.multiple_of(to_y * 64 + other * 32 + to_x * 8, 8), 8), :])
+        for h in range(2):
+            for which in range(2):
+                other = (core + which) % 2
+                for q in range(X):
+                    row = (h * 4 + to_y) * 64 + other * 32 + (x + 4 - q) % 4 * 8
+                    rows.append(pick_rows[pl.ds(pl.multiple_of(row, 8), 8), :])
         chosen = jnp.concatenate(rows, axis=0)
-        picks[to_x] = chosen.T.astype(BF16)
+        picks[to_y] = chosen.T.astype(BF16)
         chosen = chosen.astype(BF16)
         for n in range(4):
-            in_tiles(table, to_x * 1024, n, dot(chosen, feat[:, block(n)]))
-        swap_start(k, swap_out_f, swap_in_f, swaps_f[k])
-
-    select(0)
+            to_table(to_y, n, dot(chosen, feat[:, block(n)]))
+
+    g0, g1, g2, g3 = GROUPS
+    select(g0)
+    swap_start(g0, ends_f)
 
     settle("h_core")
     theirs = hub_other[...].astype(F32)[0:8]
@@ -231,24 +273,37 @@
     pl.semaphore_wait(entered.at[0], Y - 1)
     for other in z_line:
         pl.semaphore_signal(entered.at[1], inc=1, device_id=other, device_id_type=MESH)
-    select(1)
+    select(g1)
+    along_x(g0, ends_f)
+    swap_start(g1, ends_f)
     pl.semaphore_wait(entered.at[1], Z - 1)
-    post_quarter(0, swap_in_f, post_f, came_f, bounds_f[0])
-    select(2)
-
-    settle("w_z")
-    for other in x_line:
-        remote(full_weight.at[x, :, core], full_weight.at[x, :, core], w_x, other)
-    expect("w_x", full_weight.at[pl.ds(0, 3), :, 0], w_x[1])
-    leaves(full_weight.at[pl.ds(0, 3), :, 0], w_x[0])
+    post_own(g0, ends_f)
+    select(g2)
+    along_x(g1, ends_f)
+    post_own(g1, ends_f)
+    swap_start(g2, ends_f)
+    select(g3)
+    along_x(g2, ends_f)
+    post_far(g0, ends_f)
+    post_own(g2, ends_f)
+    swap_start(g3, ends_f)
+
     settle("h_z")
     y_slab = pl.ds(z_slab, 4)
     for other in y_line:
         remote(hub_tiles.at[y_slab], hub_tiles.at[y_slab], h_y, other)
     expect("h_y", hub_tiles.at[pl.ds(0, 28)], h_y[1])
     leaves(hub_tiles.at[pl.ds(0, 28)], h_y[0])
-    post_quarter(1, swap_in_f, post_f, came_f, bounds_f[1])
-    select(3)
+    along_x(g3, ends_f)
+
+    settle("w_z")
+    for other in x_line:
+        remote(full_weight.at[x, :, core], full_weight.at[x, :, core], w_x, other)
+    expect("w_x", full_weight.at[pl.ds(0, 3), :, 0], w_x[1])
+    leaves(full_weight.at[pl.ds(0, 3), :, 0], w_x[0])
+    post_far(g1, ends_f)
+    post_own(g3, ends_f)
+    post_far(g2, ends_f)
 
     settle("h_y")
     x_slab = pl.ds((x * 2 + core) * 32, 32)
@@ -256,24 +311,15 @@
         remote(hub_tiles.at[x_slab], hub_tiles.at[x_slab], h_x, other)
     expect("h_x", hub_tiles.at[pl.ds(0, 96)], h_x[1])
     leaves(hub_tiles.at[pl.ds(0, 96)], h_x[0])
-    post_quarter(2, swap_in_f, post_f, came_f, bounds_f[2])
-    post_quarter(3, swap_in_f, post_f, came_f, bounds_f[3])
-
-    settle("h_x")
-    for at in range(X):
-        slab = pl.ds((at * 2 + core) * 32, 32)
-        remote(hub_tiles.at[slab], hub_tiles.at[slab], h_last, partner)
-    expect("h_last", hub_tiles.at[pl.ds(0, 128)], h_last[1])
-    leaves(hub_tiles.at[pl.ds(0, 128)], h_last[0])
-    settle("w_x")
-    remote(full_weight.at[:, :, core], full_weight.at[:, :, core], w_core, partner)
-    expect("w_core", full_weight.at[:, :, 0], w_core[1])
-    leaves(full_weight.at[:, :, 0], w_core[0])
-
+    post_far(g3, ends_f)
+
+    loads[3].wait()
+    loads[4].wait()
     number = nbr_t[...]
     s = number - NODES
     bound_column = (
-        NODES + ((s >> 3) & 3) * 128 + (((s >> 5) + core) & 1) * 64 + (s >> 6) * 8 + (s & 7)
+        NODES + ((s >> 6) & 3) * 128 + (s >> 8) * 64 + (((s >> 5) + core) & 1) * 32
+        + ((x - (s >> 3)) & 3) * 8 + (s & 7)
     )
     h = number - (NODES + BOUND)
     hub_column = (
@@ -296,6 +342,17 @@
         rows = feat[:, block(n)]
         total[:, block(n)] = rows.astype(F32) + dot(edges[:, 0:NODES], rows)
 
+    settle("h_x")
+    for at in range(X):
+        slab = pl.ds((at * 2 + core) * 32, 32)
+        remote(hub_tiles.at[slab], hub_tiles.at[slab], h_last, partner)
+    expect("h_last", hub_tiles.at[pl.ds(0, 128)], h_last[1])
+    leaves(hub_tiles.at[pl.ds(0, 128)], h_last[0])
+    settle("w_x")
+    remote(full_weight.at[:, :, core], full_weight.at[:, :, core], w_core, partner)
+    expect("w_core", full_weight.at[:, :, 0], w_core[1])
+    leaves(full_weight.at[:, :, 0], w_core[0])
+
     settle("h_last")
     for part in range(8):
         hub_table[part * 512 : (part + 1) * 512, :] = (
@@ -305,14 +362,15 @@
         hub_lookup[:, j * 128 : (j + 1) * 128] = hub_table[pl.ds(j, HUBS, stride=8), :].astype(BF16)
     for n in range(4):
         total[:, block(n)] += dot(edges[:, NODES + BOUND : COLUMNS], hub_lookup[:, block(n)])
-    settle("w_core")
-
-    for k in range(X):
-        from_x, rows = received(k, came_f)
-        part = edges[:, pl.ds(pl.multiple_of(NODES + from_x * 128, 128), 128)]
+
+    for g in GROUPS:
+        from_y, rows = received(g, ends_f)
+        part = edges[:, pl.ds(pl.multiple_of(NODES + from_y * 128, 128), 128)]
         for n in range(4):
             total[:, block(n)] += dot(part, rows(n))
 
+    settle("w_core")
+    loads[5].wait()
     two_div = jnp.concatenate([div[...], div[...]], axis=1)
     for n in range(4):
         mean[:, block(n)] = (total[:, block(n)] / two_div).astype(BF16)
@@ -333,30 +391,34 @@
         high[:, block(n)] = top
         low[:, block(n)] = (term - top.astype(F32)).astype(BF16)
 
-    def spread(rows, ref, base):
+    def spread(rows, put):
         edge = edges_t[rows, :]
         for n in range(4):
-            in_tiles(ref, base, n, dot(edge, high[:, block(n)]) + dot(edge, low[:, block(n)]))
-
-    swaps_b = [sems() for _ in STEPS]
-    bounds_b = [sems() for _ in STEPS]
+            put(n, dot(edge, high[:, block(n)]) + dot(edge, low[:, block(n)]))
+
+    ends_b = exchange_ends(swap_out_b, swap_in_b, stage_b, mid_b, came_b)
     g_core, g_x, g_y, g_z, g_last = sems(), sems(), sems(), sems(), sems()
 
-    def give_back(k):
-        to_x = (x + STEPS[k]) % 4
-        spread(pl.ds(pl.multiple_of(NODES + to_x * 128, 128), 128), table, to_x * 1024)
-        swap_start(k, swap_out_b, swap_in_b, swaps_b[k])
-
-    give_back(0)
-
-    spread(slice(NODES + BOUND, COLUMNS), hub_table, 0)
+    def give_back(g):
+        to_y = (y + g) % 4
+        spread(
+            pl.ds(pl.multiple_of(NODES + to_y * 128, 128), 128), lambda n, part: to_table(to_y, n, part)
+        )
+        swap_start(g, ends_b)
+
+    give_back(g0)
+
+    spread(slice(NODES + BOUND, COLUMNS), lambda n, part: in_tiles(hub_table, 0, n, part))
     for at in range(X):
         slab = pl.ds(pl.multiple_of((at * 2 + 1 - core) * 512, 512), 512)
         remote(hub_table.at[slab], hub_core.at[at], g_core, partner)
     expect("g_core", hub_core, g_core[1])
     leaves(hub_core, g_core[0])
-    give_back(1)
-    post_quarter(0, swap_in_b, post_b, came_b, bounds_b[0])
+    along_x(g0, ends_b)
+    post_own(g0, ends_b)
+    give_back(g1)
+    along_x(g1, ends_b)
+    post_own(g1, ends_b)
 
     def kept(at):
         return hub_table[pl.ds(pl.multiple_of((at * 2 + core) * 512, 512), 512), :] + hub_core[at]
@@ -367,9 +429,14 @@
         remote(hub_x_out.at[d - 1], hub_x_in.at[d - 1], g_x, x_line[d - 1])
     expect("g_x", hub_x_in, g_x[1])
     leaves(hub_x_in, g_x[0])
-    give_back(2)
-    post_quarter(1, swap_in_b, post_b, came_b, bounds_b[1])
-    give_back(3)
+    post_far(g0, ends_b)
+    give_back(g2)
+    along_x(g2, ends_b)
+    post_own(g2, ends_b)
+    post_far(g1, ends_b)
+    give_back(g3)
+    along_x(g3, ends_b)
+    post_own(g3, ends_b)
 
     settle("g_x")
     part = kept(x)
@@ -381,8 +448,8 @@
         remote(hub_y_out.at[(y + d) % 8], hub_y_in.at[d - 1], g_y, y_line[d - 1])
     expect("g_y", hub_y_in, g_y[1])
     leaves(hub_y_in, g_y[0])
-    post_quarter(2, swap_in_b, post_b, came_b, bounds_b[2])
-    post_quarter(3, swap_in_b, post_b, came_b, bounds_b[3])
+    post_far(g2, ends_b)
+    post_far(g3, ends_b)
 
     for n in range(4):
         cols = block(n)
@@ -400,10 +467,10 @@
             slot = (to - z + 8) % 8 - 1
             remote(hub_y_sum.at[pl.ds(at * 16, 16)], hub_z_in.at[slot], g_z, device(y, core, x, to))
 
-    for k in range(2):
-        from_x, rows = received(k, came_b)
+    for g in (g0, g1):
+        from_y, rows = received(g, ends_b)
         for n in range(4):
-            own_sum[:, block(n)] += dot(picks[from_x], rows(n))
+            own_sum[:, block(n)] += dot(picks[from_y], rows(n))
 
     @pl.when(holds)
     def _():
@@ -428,12 +495,12 @@
         cols = slice(j * 128, (j + 1) * 128)
         own_sum[:, cols] += jnp.where(hub_mask, hub_row[j : j + 1, :], 0.0)
 
-    from_x, rows = received(2, came_b)
+    from_y, rows = received(g2, ends_b)
     for n in range(4):
-        own_sum[:, block(n)] += dot(picks[from_x], rows(n))
-    from_x, rows = received(3, came_b)
+        own_sum[:, block(n)] += dot(picks[from_y], rows(n))
+    from_y, rows = received(g3, ends_b)
     for n in range(4):
-        grad[:, block(n)] = (own_sum[:, block(n)] + dot(picks[from_x], rows(n))).astype(BF16)
+        grad[:, block(n)] = (own_sum[:, block(n)] + dot(picks[from_y], rows(n))).astype(BF16)
     for wait in sent:
         wait()
 
@@ -442,7 +509,21 @@
     return pltpu.VMEM((count, 16, 128), BF16)
 
 
+ENDS = [
+    tiles(128),
+    tiles(128),
+    pltpu.VMEM((4, X, 16, 16, 128), BF16),
+    pltpu.VMEM((4, X - 1, 16, 16, 128), BF16),
+    pltpu.VMEM((Y, X, Z, 16, 128), BF16),
+]
+
 SCRATCH = [
+    pltpu.VMEM((NODES, WIDTH), BF16),
+    pltpu.VMEM((NODES, WIDTH), BF16),
+    pltpu.VMEM((32, WIDTH), BF16),
+    pltpu.VMEM((16, NODES), I32),
+    pltpu.VMEM((1, NODES), I32),
+    pltpu.VMEM((1, BOUND), I32),
     pltpu.VMEM((BOUND, NODES), F32),
     pltpu.VMEM((X, NODES, 128), BF16),
     pltpu.VMEM((4096, 128), F32),
@@ -459,8 +540,8 @@
     pltpu.VMEM((NODES, WIDTH), BF16),
     pltpu.VMEM((NODES, WIDTH), BF16),
     pltpu.VMEM((NODES, WIDTH), F32),
-    tiles(128), tiles(128), tiles(256), tiles(256),
-    tiles(128), tiles(128), tiles(256), tiles(256),
+    *ENDS,
+    *ENDS,
     pltpu.VMEM((16, 128), BF16),
     pltpu.VMEM((16, 128), BF16),
     tiles(256),
@@ -476,14 +557,16 @@
     pltpu.VMEM((16, 128), F32),
     pltpu.VMEM((16, 128), F32),
     pltpu.VMEM((8, 128), F32),
-    pltpu.SemaphoreType.DMA((32,)),
-    pltpu.SemaphoreType.DMA((32,)),
+    pltpu.SemaphoreType.DMA((48,)),
+    pltpu.SemaphoreType.DMA((48,)),
+    pltpu.SemaphoreType.DMA((6,)),
     pltpu.SemaphoreType.REGULAR((2,)),
 ]
 
 
 def on_device(feat, cotangent, weight, nbr_index, degree, send_rows, hub_rows):
     vmem = pl.BlockSpec(memory_space=pltpu.VMEM)
+    hbm = pl.BlockSpec(memory_space=pltpu.HBM)
     smem = pl.BlockSpec(memory_space=pltpu.SMEM)
     return pl.pallas_call(
         whole_kernel,
@@ -491,10 +574,10 @@
             jax.ShapeDtypeStruct((NODES, WIDTH), BF16),
             jax.ShapeDtypeStruct((NODES, WIDTH), BF16),
         ),
-        in_specs=[vmem] * 6 + [smem],
+        in_specs=[hbm] * 6 + [smem],
         out_specs=(vmem, vmem),
         scratch_shapes=SCRATCH,
-        compiler_params=pltpu.CompilerParams(has_side_effects=True, collective_id=0, vmem_limit_bytes=48 << 20),
+        compiler_params=pltpu.CompilerParams(has_side_effects=True, collective_id=0, vmem_limit_bytes=63 << 20),
         name="sage",
     )(feat, cotangent, weight, nbr_index.T, degree[None, :], send_rows.T, hub_rows)
 

time: 106 us -> 97.2 us (0.917)
  Pallas kernels: 99.1 us -> 92.8 us
  local copies, waits for them, and re-layouts: 5.51 us -> 2.42 us
    pallas_call x1, Pallas kernels: 99.1 us -> 92.8 us  [on_device(): pl.pallas_call(whole_kernel, out_shape=(jax.ShapeDtypeStruct((NODES, WIDT...]
    unnamed x14 -> x4, local copies, waits for them, and re-layouts: 5.51 us -> 2.42 us
where the time goes in v4:
time: 97.2 us; the launch traced here: 96.5 us
  Pallas kernels  92.8 us (95%)
  local copies, waits for them, and re-layouts  2.42 us (2%)
  between operations  1.3 us (1%)
    pallas_call x1, Pallas kernels, on_device(): pl.pallas_call(whole_kernel, out_shape=(jax.ShapeDtypeStruct((NODES, WIDT...  92.8 us
    unnamed x4, local copies, waits for them, and re-layouts  2.42 us

profile of v4, /device:TPU:1, one launch (start us, length us, event | category | flops | bytes accessed | tf_op | source)
XLA Modules:
  0.0 96.5 jit_solution(240397268084680786)
XLA Ops:
  1.3 92.8 %sage.1 = (bf16[128,1024]{1,0:T(8,128)(2,1)}, bf16[128,1024]{1,0:T(8,128)(2,1)}) custom-call(bf16[128,1024]{1,0:T(8,128)(2,1)} %feat_hbm.1, bf16[128,1024]{1,0:T(8,128)(2,1)} %cot_hbm.1, bf16[32,1024]{1,0:T(8,128)(2,1)} %shard_hbm.1, s32[16,128]{1,0:T(8,128)} %bitcast.3, s32[1,128]{1,0:T(1,128)} %bitcast.5, s32[1,512]{1,0:T(1,128)} %bitcast.4, s32[1]{0:T(128)S(6)} %copy.11.hub_at), custom_call_target="tpu_custom_call" | custom-call | tf_op jit(solution)/shard_map/sage/pallas_call | solution.py:571
  94.1 0.0 copy-start
  94.1 1.7 %copy.12 = bf16[128,1024]{1,0:T(8,128)(2,1)} copy(bf16[128,1024]{1,0:T(8,128)(2,1)} %get-tuple-element.4) | data formatting | bytes 524288
  95.8 0.0 copy-done
  95.8 0.7 copy.13
Async XLA Ops:
  94.1 1.7 %copy-start = (bf16[128,1024]{1,0:T(8,128)(2,1)S(1)}, bf16[128,1024]{1,0:T(8,128)(2,1)}, u32[]{:S(2)}) copy-start(bf16[128,1024]{1,0:T(8,128)(2,1)} %get-tuple-element.5) | copy-start | bytes 786436

commit v5 on v4

--- a/solution.py
+++ b/solution.py
@@ -8,8 +8,6 @@
 MESH = pl.DeviceIdType.MESH
 BF16, F32, I32 = jnp.bfloat16, jnp.float32, jnp.int32
 Y, X, Z = 8, 4, 8
-CHIPS = Y * X * Z
-PLANE = Y * Z
 NODES, WIDTH, BOUND, HUBS = 128, 1024, 512, 512
 COLUMNS = NODES + BOUND + HUBS
 GROUPS = (2, 1, 3, 0)
@@ -101,24 +99,6 @@
     for j in range(8):
         own_hub = jnp.where(lane_group == j, hub_wide[:, j * 128 : (j + 1) * 128], own_hub)
     hub_tile[...] = jnp.concatenate([own_hub, own_hub], axis=0).astype(BF16)
-    loads[2].wait()
-    pl.semaphore_wait(barrier, len(x_line) + len(y_line) + len(z_line) + 1)
-
-    w_z, w_x, w_core = sems(), sems(), sems()
-    half = pl.ds(pl.multiple_of(core * 16, 16), 16)
-    for other in z_line:
-        remote(shard.at[half], full_weight.at[x, z, core], w_z, other)
-    expect("w_z", full_weight.at[0, pl.ds(0, 7), 0], w_z[1])
-    leaves(full_weight.at[0, pl.ds(0, 7), 0], w_z[0])
-    for other in y_line:
-        pl.semaphore_signal(entered.at[0], inc=1, device_id=other, device_id_type=MESH)
-    h_core, h_z, h_y, h_x, h_last = sems(), sems(), sems(), sems(), sems()
-    remote(hub_tile, hub_other, h_core, partner)
-    expect("h_core", hub_other, h_core[1])
-    leaves(hub_tile, h_core[0])
-    full_weight[x, z, 0] = shard[0:16]
-    full_weight[x, z, 1] = shard[16:32]
-
     def in_tiles(ref, base, n, part):
         for e in range(2):
             ref[pl.ds(base + 2 * n + e, part.shape[0], stride=8), :] = part[:, e * 128 : (e + 1) * 128]
@@ -127,8 +107,8 @@
         row = ((y + g + i // 8 * 4) % 8) * 64 + which * 32 + (4 - dx) % 4 * 8 + (z + i) % 8
         return table[pl.ds(pl.multiple_of(row * 8, 8), 8), :]
 
-    def swap_start(g, ends):
-        swap_out, swap_in, pair = ends["swap_out"], ends["swap_in"], ends["swap"][g]
+    def swap_build(g, ends):
+        swap_out = ends["swap_out"]
         for dx in range(X):
 
             def build(m, carry):
@@ -137,6 +117,9 @@
                 return carry
 
             lax.fori_loop(0, 8, build, 0, unroll=4)
+
+    def swap_send(g, ends):
+        swap_out, swap_in, pair = ends["swap_out"], ends["swap_in"], ends["swap"][g]
         part = pl.ds(g * 32, 32)
         remote(swap_out.at[part], swap_in.at[part], pair, partner)
         expect(("swap", g), swap_in.at[part], pair[1])
@@ -239,7 +222,26 @@
 
     g0, g1, g2, g3 = GROUPS
     select(g0)
-    swap_start(g0, ends_f)
+    swap_build(g0, ends_f)
+    select(g1)
+    loads[2].wait()
+    pl.semaphore_wait(barrier, len(x_line) + len(y_line) + len(z_line) + 1)
+    for d in range(1, Y):
+        pl.semaphore_signal(entered.at[Y - d], inc=1, device_id=y_line[d - 1], device_id_type=MESH)
+    swap_send(g0, ends_f)
+
+    w_z, w_x, w_core = sems(), sems(), sems()
+    half = pl.ds(pl.multiple_of(core * 16, 16), 16)
+    for other in z_line:
+        remote(shard.at[half], full_weight.at[x, z, core], w_z, other)
+    expect("w_z", full_weight.at[0, pl.ds(0, 7), 0], w_z[1])
+    leaves(full_weight.at[0, pl.ds(0, 7), 0], w_z[0])
+    h_core, h_z, h_y, h_x, h_last = sems(), sems(), sems(), sems(), sems()
+    remote(hub_tile, hub_other, h_core, partner)
+    expect("h_core", hub_other, h_core[1])
+    leaves(hub_tile, h_core[0])
+    full_weight[x, z, 0] = shard[0:16]
+    full_weight[x, z, 1] = shard[16:32]
 
     settle("h_core")
     theirs = hub_other[...].astype(F32)[0:8]
@@ -270,23 +272,30 @@
 
     due["h_z"] = hub_z_due
     sent.append(hub_z_left)
-    pl.semaphore_wait(entered.at[0], Y - 1)
-    for other in z_line:
-        pl.semaphore_signal(entered.at[1], inc=1, device_id=other, device_id_type=MESH)
-    select(g1)
     along_x(g0, ends_f)
-    swap_start(g1, ends_f)
-    pl.semaphore_wait(entered.at[1], Z - 1)
+    swap_build(g1, ends_f)
+    swap_send(g1, ends_f)
+
+    def greeted(g):
+        for dy in (g, g + 4):
+            if dy:
+                pl.semaphore_wait(entered.at[dy], 1)
+
+    greeted(g0)
     post_own(g0, ends_f)
     select(g2)
     along_x(g1, ends_f)
+    greeted(g1)
     post_own(g1, ends_f)
-    swap_start(g2, ends_f)
+    swap_build(g2, ends_f)
+    swap_send(g2, ends_f)
     select(g3)
     along_x(g2, ends_f)
     post_far(g0, ends_f)
+    greeted(g2)
     post_own(g2, ends_f)
-    swap_start(g3, ends_f)
+    swap_build(g3, ends_f)
+    swap_send(g3, ends_f)
 
     settle("h_z")
     y_slab = pl.ds(z_slab, 4)
@@ -302,6 +311,7 @@
     expect("w_x", full_weight.at[pl.ds(0, 3), :, 0], w_x[1])
     leaves(full_weight.at[pl.ds(0, 3), :, 0], w_x[0])
     post_far(g1, ends_f)
+    greeted(g3)
     post_own(g3, ends_f)
     post_far(g2, ends_f)
 
@@ -404,9 +414,14 @@
         spread(
             pl.ds(pl.multiple_of(NODES + to_y * 128, 128), 128), lambda n, part: to_table(to_y, n, part)
         )
-        swap_start(g, ends_b)
+        swap_build(g, ends_b)
+        swap_send(g, ends_b)
 
     give_back(g0)
+
+    give_back(g1)
+    along_x(g0, ends_b)
+    post_own(g0, ends_b)
 
     spread(slice(NODES + BOUND, COLUMNS), lambda n, part: in_tiles(hub_table, 0, n, part))
     for at in range(X):
@@ -414,11 +429,9 @@
         remote(hub_table.at[slab], hub_core.at[at], g_core, partner)
     expect("g_core", hub_core, g_core[1])
     leaves(hub_core, g_core[0])
-    along_x(g0, ends_b)
-    post_own(g0, ends_b)
-    give_back(g1)
     along_x(g1, ends_b)
     post_own(g1, ends_b)
+    give_back(g2)
 
     def kept(at):
         return hub_table[pl.ds(pl.multiple_of((at * 2 + core) * 512, 512), 512), :] + hub_core[at]
@@ -430,11 +443,10 @@
     expect("g_x", hub_x_in, g_x[1])
     leaves(hub_x_in, g_x[0])
     post_far(g0, ends_b)
-    give_back(g2)
     along_x(g2, ends_b)
     post_own(g2, ends_b)
+    give_back(g3)
     post_far(g1, ends_b)
-    give_back(g3)
     along_x(g3, ends_b)
     post_own(g3, ends_b)
 
@@ -560,7 +572,7 @@
     pltpu.SemaphoreType.DMA((48,)),
     pltpu.SemaphoreType.DMA((48,)),
     pltpu.SemaphoreType.DMA((6,)),
-    pltpu.SemaphoreType.REGULAR((2,)),
+    pltpu.SemaphoreType.REGULAR((Y,)),
 ]
 
 

time: 97.2 us -> 95 us (0.977)
  Pallas kernels: 92.8 us -> 91.1 us
    pallas_call x1, Pallas kernels: 92.8 us -> 91.1 us  [on_device(): pl.pallas_call(whole_kernel, out_shape=(jax.ShapeDtypeStruct((NODES, WIDT...]
where the time goes in v5:
time: 95 us; the launch traced here: 94.8 us
  Pallas kernels  91.1 us (96%)
  local copies, waits for them, and re-layouts  2.42 us (3%)
  between operations  1.3 us (1%)
    pallas_call x1, Pallas kernels, on_device(): pl.pallas_call(whole_kernel, out_shape=(jax.ShapeDtypeStruct((NODES, WIDT...  91.1 us
    unnamed x4, local copies, waits for them, and re-layouts  2.42 us

profile of v5, /device:TPU:1, one launch (start us, length us, event | category | flops | bytes accessed | tf_op | source)
XLA Modules:
  0.0 94.8 jit_solution(17382012388116189999)
XLA Ops:
  1.3 91.1 %sage.1 = (bf16[128,1024]{1,0:T(8,128)(2,1)}, bf16[128,1024]{1,0:T(8,128)(2,1)}) custom-call(bf16[128,1024]{1,0:T(8,128)(2,1)} %feat_hbm.1, bf16[128,1024]{1,0:T(8,128)(2,1)} %cot_hbm.1, bf16[32,1024]{1,0:T(8,128)(2,1)} %shard_hbm.1, s32[16,128]{1,0:T(8,128)} %bitcast.3, s32[1,128]{1,0:T(1,128)} %bitcast.5, s32[1,512]{1,0:T(1,128)} %bitcast.4, s32[1]{0:T(128)S(6)} %copy.11.hub_at), custom_call_target="tpu_custom_call" | custom-call | tf_op jit(solution)/shard_map/sage/pallas_call | solution.py:583
  92.4 0.0 copy-start
  92.4 1.7 %copy.12 = bf16[128,1024]{1,0:T(8,128)(2,1)} copy(bf16[128,1024]{1,0:T(8,128)(2,1)} %get-tuple-element.4) | data formatting | bytes 524288
  94.1 0.0 copy-done
  94.1 0.7 copy.13
Async XLA Ops:
  92.4 1.7 %copy-start = (bf16[128,1024]{1,0:T(8,128)(2,1)S(1)}, bf16[128,1024]{1,0:T(8,128)(2,1)}, u32[]{:S(2)}) copy-start(bf16[128,1024]{1,0:T(8,128)(2,1)} %get-tuple-element.5) | copy-start | bytes 786436

commit v6 on v5

--- a/solution.py
+++ b/solution.py
@@ -538,8 +538,8 @@
     pltpu.VMEM((1, BOUND), I32),
     pltpu.VMEM((BOUND, NODES), F32),
     pltpu.VMEM((X, NODES, 128), BF16),
-    pltpu.VMEM((4096, 128), F32),
-    pltpu.VMEM((1024, 128), F32),
+    pltpu.VMEM((4104, 128), F32),
+    pltpu.VMEM((1040, 128), F32),
     pltpu.VMEM((X, Z, 2, 16, WIDTH), BF16),
     pltpu.VMEM((NODES, COLUMNS), BF16),
     pltpu.VMEM((COLUMNS, NODES), BF16),
@@ -557,7 +557,7 @@
     pltpu.VMEM((16, 128), BF16),
     pltpu.VMEM((16, 128), BF16),
     tiles(256),
-    pltpu.VMEM((4096, 128), F32),
+    pltpu.VMEM((4104, 128), F32),
     pltpu.VMEM((X, 512, 128), F32),
     pltpu.VMEM((X - 1, 512, 128), BF16),
     pltpu.VMEM((X - 1, 512, 128), BF16),

time: 95 us -> 95 us (level)
  no operation moved by 1% of the time
where the time goes in v6:
time: 95 us; the launch traced here: 94.9 us
  Pallas kernels  91.2 us (96%)
  local copies, waits for them, and re-layouts  2.42 us (3%)
  between operations  1.3 us (1%)
    pallas_call x1, Pallas kernels, on_device(): pl.pallas_call(whole_kernel, out_shape=(jax.ShapeDtypeStruct((NODES, WIDT...  91.2 us
    unnamed x4, local copies, waits for them, and re-layouts  2.42 us

profile of v6, /device:TPU:1, one launch (start us, length us, event | category | flops | bytes accessed | tf_op | source)
XLA Modules:
  0.0 94.9 jit_solution(6394996641179647807)
XLA Ops:
  1.3 91.2 %sage.1 = (bf16[128,1024]{1,0:T(8,128)(2,1)}, bf16[128,1024]{1,0:T(8,128)(2,1)}) custom-call(bf16[128,1024]{1,0:T(8,128)(2,1)} %feat_hbm.1, bf16[128,1024]{1,0:T(8,128)(2,1)} %cot_hbm.1, bf16[32,1024]{1,0:T(8,128)(2,1)} %shard_hbm.1, s32[16,128]{1,0:T(8,128)} %bitcast.3, s32[1,128]{1,0:T(1,128)} %bitcast.5, s32[1,512]{1,0:T(1,128)} %bitcast.4, s32[1]{0:T(128)S(6)} %copy.11.hub_at), custom_call_target="tpu_custom_call" | custom-call | tf_op jit(solution)/shard_map/sage/pallas_call | solution.py:583
  92.4 0.0 copy-start
  92.4 1.7 %copy.12 = bf16[128,1024]{1,0:T(8,128)(2,1)} copy(bf16[128,1024]{1,0:T(8,128)(2,1)} %get-tuple-element.4) | data formatting | bytes 524288
  94.2 0.0 copy-done
  94.2 0.7 copy.13
Async XLA Ops:
  92.4 1.7 %copy-start = (bf16[128,1024]{1,0:T(8,128)(2,1)S(1)}, bf16[128,1024]{1,0:T(8,128)(2,1)}, u32[]{:S(2)}) copy-start(bf16[128,1024]{1,0:T(8,128)(2,1)} %get-tuple-element.5) | copy-start | bytes 786436
